TPU v7x, 32 devices: a whole 2x2x4 slice. The times are simulated.
32 devices in a mesh: parts: 2 (over x), lon: 16 (over z, y, core).
Axes of the slice: x: 2, y: 2, z: 4, core: 2. Of those that a mesh axis runs over, the one named last changes fastest.
Arguments:
- state: bfloat16 [128, 256, 512], P('parts', 'lon'), parts along dimension 0, may hold values from -6 to 6
- zonal_width: int32 [64], replicated, may hold values from 1 to 32, as said below
- tap_rows: int32 [64, 3], replicated, may hold values from 0 to 63, as said below
- filters: bfloat16 [2, 8, 64, 3, 65], replicated, may hold values from -0.875 to 0.875
- basis_mix: float32 [2, 8, 512], replicated, may hold values from -2 to 2
- norm_gain: float32 [2, 512], replicated, may hold values from 0.1 to 1.9
- weight_in: bfloat16 [2, 512, 1024], replicated, may hold values from -0.25 to 0.25
- bias_in: float32 [2, 1024], replicated, may hold values from -3 to 3
- weight_out: bfloat16 [2, 1024, 512], replicated, may hold values from -0.1875 to 0.1875
Outputs:
- advanced: bfloat16 [128, 256, 512], P('parts', 'lon'), parts along dimension 0
There are 2 independent parts, one for each index of `parts`. A program takes and returns all parts, laid end to end along the dimension named above; an argument that names none is the same for every part. Nothing has to cross between parts.
Inputs may be any that keep to these rules, and one draw needn't show every extreme that they name: `zonal_width`: rows i with 16 <= i < 48 have widths of at most 16, and one of them has exactly 16; the first and last rows have 32. `tap_rows`: each entry differs from its own row index by at most 2.
All inputs are finite; a program needn't handle non-finite values.
Results may differ from a plain program's by a relative error of at most 0.0059.
Values may be sent and summed in bfloat16 or wider, within the bound.
A program may use at most 64 MiB of HBM per device.

v0:
```python
import jax
import jax.numpy as jnp
from jax import lax
from jax.sharding import PartitionSpec as P


def shifted(block, axis, distance):
    devices = range(lax.axis_size(axis))
    route = [((i - distance) % len(devices), i) for i in devices]
    return lax.ppermute(block, axis, route)


def layer_norm(filtered, gain):
    row_mean = jnp.mean(filtered, axis=-1, keepdims=True)
    centred = filtered - row_mean
    row_var = jnp.mean(centred * centred, axis=-1, keepdims=True)
    return (centred / jnp.sqrt(row_var + 1e-05) * gain).astype(jnp.bfloat16)


def neighbour_strips(current):
    near_west = shifted(current, "lon", 1)
    near_east = shifted(current, "lon", -1)
    west_list = [near_west]
    east_list = [near_east]
    west_piece = shifted(current, "lon", 2)
    east_piece = shifted(current, "lon", -2)
    west_list = [west_piece] + west_list
    east_list = east_list + [east_piece]
    return jnp.concatenate(west_list + [current] + east_list, axis=1)


def disco_strip(widened, tap_rows, filter_set, mix_set, zonal_width, lon_dev):
    lat_rows, span_cells, channels = widened.shape
    basis_count, _, tap_count, offset_count = filter_set.shape
    half_span = (offset_count - 1) // 2
    blocks = 4
    block_rows = lat_rows // blocks
    window_rows = block_rows + 4
    offset_ids = jnp.arange(offset_count, dtype=jnp.int32)
    out_ids = jnp.arange(lon_dev, dtype=jnp.int32)
    span_ids = jnp.arange(span_cells, dtype=jnp.int32)
    band_table = span_ids[None, None, :] - out_ids[None, :, None] == offset_ids[:, None, None]
    band_table = band_table.astype(jnp.bfloat16).reshape(offset_count, lon_dev * span_cells)
    window_ids = jnp.arange(window_rows, dtype=jnp.int32)

    def one_block(block_id):
        row_start = block_id * block_rows
        filter_block = lax.dynamic_slice_in_dim(filter_set, row_start, block_rows, axis=1)
        width_block = lax.dynamic_slice_in_dim(zonal_width, row_start, block_rows, axis=0)
        tap_block = lax.dynamic_slice_in_dim(tap_rows, row_start, block_rows, axis=0)
        in_support = jnp.abs(offset_ids - half_span)[None, :] <= width_block[:, None]
        masked = jnp.where(
            in_support[None, :, None, :], filter_block, jnp.zeros((), filter_block.dtype)
        )
        banded = jnp.dot(
            masked.reshape(-1, offset_count), band_table, preferred_element_type=jnp.float32
        )
        banded = banded.astype(jnp.bfloat16).reshape(
            basis_count, block_rows, tap_count, lon_dev, span_cells
        )
        window_start = jnp.clip(row_start - 2, 0, lat_rows - window_rows)
        window = lax.dynamic_slice_in_dim(widened, window_start, window_rows, axis=0)
        selector = (tap_block[:, :, None] == (window_start + window_ids)[None, None, :]).astype(
            jnp.bfloat16
        )
        picked = jnp.einsum(
            "itr,rmc->itmc", selector, window, preferred_element_type=jnp.float32
        ).astype(jnp.bfloat16)
        basis_terms = jnp.einsum(
            "kitjm,itmc->kijc", banded, picked, preferred_element_type=jnp.float32
        )
        return jnp.sum(mix_set[:, None, None, :] * basis_terms, axis=0)

    filtered = lax.map(one_block, jnp.arange(blocks, dtype=jnp.int32))
    return filtered.reshape(lat_rows, lon_dev, channels)


def per_device(
    state, zonal_width, tap_rows, filters, basis_mix, norm_gain, weight_in, bias_in, weight_out
):
    lat_rows, lon_dev, channels = state.shape
    layer_count = filters.shape[0]
    current = state
    for layer_index in range(layer_count):
        widened = neighbour_strips(current)
        filtered = disco_strip(
            widened, tap_rows, filters[layer_index], basis_mix[layer_index], zonal_width, lon_dev
        )
        normed = layer_norm(filtered, norm_gain[layer_index])
        flat_rows = normed.reshape(lat_rows * lon_dev, channels)
        pre_act = jnp.dot(flat_rows, weight_in[layer_index], preferred_element_type=jnp.float32)
        hidden = jax.nn.gelu(pre_act + bias_in[layer_index], approximate=True).astype(jnp.bfloat16)
        update = jnp.dot(hidden, weight_out[layer_index], preferred_element_type=jnp.float32)
        current = (
            current.astype(jnp.float32) + update.reshape(lat_rows, lon_dev, channels)
        ).astype(jnp.bfloat16)
    return current


def solution(mesh):
    placed = (P("parts", "lon", None), P(), P(), P(), P(), P(), P(), P(), P())
    return jax.shard_map(
        per_device, mesh=mesh, in_specs=placed, out_specs=P("parts", "lon", None), check_vma=False
    )
```

profile of v0, /device:TPU:0, one launch (start us, length us, event | category | flops | bytes accessed | tf_op | source)
XLA Modules:
  0.0 306.2 jit_solution(4913886838904975324)
XLA Ops:
  0.0 3.0 collective-permute-start
  3.0 4.4 %collective-permute-start.2 = (bf16[64,16,512]{2,1,0:T(8,128)(2,1)}, bf16[64,16,512]{2,1,0:T(8,128)(2,1)S(1)}, u32[]{:S(2)}, u32[]{:S(2)}) collective-permute-start(bf16[64,16,512]{2,1,0:T(8,128)(2,1)} %param.13), channel_id=1, source_target_pairs={{1,0},{2,1},{3,2},{4,3},{5,4},{6,5},{7,6},{8,7},{9,8},{10,9},{11,1... | collective-permute-start | bytes 3145736 | tf_op jit(solution)/shard_map/ppermute | solution.py:10
  10.2 50.3 %collective-permute-done = bf16[64,16,512]{2,1,0:T(8,128)(2,1)} collective-permute-done((bf16[64,16,512]{2,1,0:T(8,128)(2,1)}, bf16[64,16,512]{2,1,0:T(8,128)(2,1)}, u32[]{:S(2)}, u32[]{:S(2)}) %collective-permute-start) | collective-permute-done | bytes 1048608 | tf_op jit(solution)/shard_map/ppermute | solution.py:10
  63.4 11.0 %collective-permute-done.3 = bf16[64,16,512]{2,1,0:T(8,128)(2,1)S(1)} collective-permute-done((bf16[64,16,512]{2,1,0:T(8,128)(2,1)}, bf16[64,16,512]{2,1,0:T(8,128)(2,1)S(1)}, u32[]{:S(2)}, u32[]{:S(2)}) %collective-permute-start.3) | collective-permute-done | bytes 1048608 | tf_op jit(solution)/shard_map/ppermute | solution.py:10
  77.4 69.5 %while.26 = (s32[]{:T(128)}, f32[4,16,16,512]{3,2,1,0:T(8,128)}, f32[1,8,512]{2,1,0:T(8,128)S(1)}, s32[4]{0:T(128)S(1)}, s32[64,3]{0,1:T(4,128)S(1)}, /*index=5*...) while((s32[]{:T(128)}, f32[4,16,16,512]{3,2,1,0:T(8,128)}, ...), condition=%wide.region_2.3_spmd.clone, body=%wide.region_0.2_spmd.clone.sunk | while | flops 648508416 | bytes 18561748 | solution.py:74
  80.5 3.6 %fusion.98 = bf16[16,3,80,512]{3,0,2,1:T(8,128)(2,1)} fusion(bf16[20,80,512,1]{2,1,0,3:T(8,128)(2,1)S(1)} %dynamic-slice_bitcast_fusion.4, pred[16,3,20,1]{2,1,0,3:T(4,128)(4,1)S(1)} %compare_bitcast_fusion.4), kind=kOutput, calls=%fused_computation.12.clone.1 | convolution fusion | flops 78643200 | bytes 5571520 | tf_op jit(solution)/shard_map/while/body/eval_jaxpr/itr,rmc->itmc/dot_general | solution.py:66
  84.8 2.4 reshape.235
  87.2 6.7 %fusion.100 = f32[16,16,512]{2,1,0:T(8,128)S(1)} fusion(f32[8,512]{1,0:T(8,128)S(1)} %bitcast.115, bf16[16,3,80,512]{3,0,2,1:T(8,128)(2,1)} %fusion.98, bf16[8,16,3,16,80]{4,3,2,1,0:T(8,128)(2,1)S(1)} %reshape.235), kind=kOutput, calls=%fused_computation.8.clone.1 | convolution fusion | flops 505282560 | bytes 5455872 | tf_op jit(solution)/shard_map/while/body/eval_jaxpr/kitjm,itmc->kijc/dot_general | solution.py:69
  97.8 3.6 %fusion.98 = bf16[16,3,80,512]{3,0,2,1:T(8,128)(2,1)} fusion(bf16[20,80,512,1]{2,1,0,3:T(8,128)(2,1)S(1)} %dynamic-slice_bitcast_fusion.4, pred[16,3,20,1]{2,1,0,3:T(4,128)(4,1)S(1)} %compare_bitcast_fusion.4), kind=kOutput, calls=%fused_computation.12.clone.1 | convolution fusion | flops 78643200 | bytes 5571520 | tf_op jit(solution)/shard_map/while/body/eval_jaxpr/itr,rmc->itmc/dot_general | solution.py:66
  102.1 2.4 reshape.235
  104.6 6.7 %fusion.100 = f32[16,16,512]{2,1,0:T(8,128)S(1)} fusion(f32[8,512]{1,0:T(8,128)S(1)} %bitcast.115, bf16[16,3,80,512]{3,0,2,1:T(8,128)(2,1)} %fusion.98, bf16[8,16,3,16,80]{4,3,2,1,0:T(8,128)(2,1)S(1)} %reshape.235), kind=kOutput, calls=%fused_computation.8.clone.1 | convolution fusion | flops 505282560 | bytes 5455872 | tf_op jit(solution)/shard_map/while/body/eval_jaxpr/kitjm,itmc->kijc/dot_general | solution.py:69
  115.2 3.6 %fusion.98 = bf16[16,3,80,512]{3,0,2,1:T(8,128)(2,1)} fusion(bf16[20,80,512,1]{2,1,0,3:T(8,128)(2,1)S(1)} %dynamic-slice_bitcast_fusion.4, pred[16,3,20,1]{2,1,0,3:T(4,128)(4,1)S(1)} %compare_bitcast_fusion.4), kind=kOutput, calls=%fused_computation.12.clone.1 | convolution fusion | flops 78643200 | bytes 5571520 | tf_op jit(solution)/shard_map/while/body/eval_jaxpr/itr,rmc->itmc/dot_general | solution.py:66
  119.5 2.4 reshape.235
  122.0 6.7 %fusion.100 = f32[16,16,512]{2,1,0:T(8,128)S(1)} fusion(f32[8,512]{1,0:T(8,128)S(1)} %bitcast.115, bf16[16,3,80,512]{3,0,2,1:T(8,128)(2,1)} %fusion.98, bf16[8,16,3,16,80]{4,3,2,1,0:T(8,128)(2,1)S(1)} %reshape.235), kind=kOutput, calls=%fused_computation.8.clone.1 | convolution fusion | flops 505282560 | bytes 5455872 | tf_op jit(solution)/shard_map/while/body/eval_jaxpr/kitjm,itmc->kijc/dot_general | solution.py:69
  132.6 3.6 %fusion.98 = bf16[16,3,80,512]{3,0,2,1:T(8,128)(2,1)} fusion(bf16[20,80,512,1]{2,1,0,3:T(8,128)(2,1)S(1)} %dynamic-slice_bitcast_fusion.4, pred[16,3,20,1]{2,1,0,3:T(4,128)(4,1)S(1)} %compare_bitcast_fusion.4), kind=kOutput, calls=%fused_computation.12.clone.1 | convolution fusion | flops 78643200 | bytes 5571520 | tf_op jit(solution)/shard_map/while/body/eval_jaxpr/itr,rmc->itmc/dot_general | solution.py:66
  136.9 2.4 reshape.235
  139.3 6.7 %fusion.100 = f32[16,16,512]{2,1,0:T(8,128)S(1)} fusion(f32[8,512]{1,0:T(8,128)S(1)} %bitcast.115, bf16[16,3,80,512]{3,0,2,1:T(8,128)(2,1)} %fusion.98, bf16[8,16,3,16,80]{4,3,2,1,0:T(8,128)(2,1)S(1)} %reshape.235), kind=kOutput, calls=%fused_computation.8.clone.1 | convolution fusion | flops 505282560 | bytes 5455872 | tf_op jit(solution)/shard_map/while/body/eval_jaxpr/kitjm,itmc->kijc/dot_general | solution.py:69
  154.8 4.4 %collective-permute-start.6 = (bf16[64,16,512]{2,1,0:T(8,128)(2,1)S(1)}, bf16[64,16,512]{2,1,0:T(8,128)(2,1)}, u32[]{:S(2)}, u32[]{:S(2)}) collective-permute-start(bf16[64,16,512]{2,1,0:T(8,128)(2,1)S(1)} %add_convert_fusion.1), channel_id=1, source_target_pairs={{1,0},{2,1},{3,2},{4,3},{5,4},{6,5},{7,6},{8,7},{9,8},{10,9},{11,1... | collective-permute-start | bytes 3145736 | tf_op jit(solution)/shard_map/ppermute | solution.py:10
  161.3 50.8 %collective-permute-done.4 = bf16[64,16,512]{2,1,0:T(8,128)(2,1)} collective-permute-done((bf16[64,16,512]{2,1,0:T(8,128)(2,1)S(1)}, bf16[64,16,512]{2,1,0:T(8,128)(2,1)}, u32[]{:S(2)}, u32[]{:S(2)}) %collective-permute-start.4) | collective-permute-done | bytes 1048608 | tf_op jit(solution)/shard_map/ppermute | solution.py:10
  216.1 9.0 %collective-permute-done.7 = bf16[64,16,512]{2,1,0:T(8,128)(2,1)S(1)} collective-permute-done((bf16[64,16,512]{2,1,0:T(8,128)(2,1)S(1)}, bf16[64,16,512]{2,1,0:T(8,128)(2,1)S(1)}, u32[]{:S(2)}, u32[]{:S(2)}) %collective-permute-start.7) | collective-permute-done | bytes 1048608 | tf_op jit(solution)/shard_map/ppermute | solution.py:10
  228.2 69.5 %while.27 = (s32[]{:T(128)}, f32[4,16,16,512]{3,2,1,0:T(8,128)}, f32[1,8,512]{2,1,0:T(8,128)S(1)}, s32[4]{0:T(128)S(1)}, s32[64,3]{0,1:T(4,128)S(1)}, /*index=5*...) while((s32[]{:T(128)}, f32[4,16,16,512]{3,2,1,0:T(8,128)}, ...), condition=%wide.region_7.8_spmd.clone, body=%wide.region_5.7_spmd.clone.sunk | while | flops 648508416 | bytes 18561748 | solution.py:74
  231.3 3.6 %fusion.107 = bf16[16,3,80,512]{3,0,2,1:T(8,128)(2,1)} fusion(bf16[20,80,512,1]{2,1,0,3:T(8,128)(2,1)S(1)} %dynamic-slice_bitcast_fusion.5, pred[16,3,20,1]{2,1,0,3:T(4,128)(4,1)S(1)} %compare_bitcast_fusion.5), kind=kOutput, calls=%fused_computation.34.clone.1 | convolution fusion | flops 78643200 | bytes 5571520 | tf_op jit(solution)/shard_map/while/body/eval_jaxpr/itr,rmc->itmc/dot_general | solution.py:66
  235.6 2.4 reshape.237
  238.0 6.7 %fusion.109 = f32[16,16,512]{2,1,0:T(8,128)S(1)} fusion(f32[8,512]{1,0:T(8,128)S(1)} %bitcast.114, bf16[16,3,80,512]{3,0,2,1:T(8,128)(2,1)} %fusion.107, bf16[8,16,3,16,80]{4,3,2,1,0:T(8,128)(2,1)S(1)} %reshape.237), kind=kOutput, calls=%fused_computation.30.clone.1 | convolution fusion | flops 505282560 | bytes 5455872 | tf_op jit(solution)/shard_map/while/body/eval_jaxpr/kitjm,itmc->kijc/dot_general | solution.py:69
  248.6 3.6 %fusion.107 = bf16[16,3,80,512]{3,0,2,1:T(8,128)(2,1)} fusion(bf16[20,80,512,1]{2,1,0,3:T(8,128)(2,1)S(1)} %dynamic-slice_bitcast_fusion.5, pred[16,3,20,1]{2,1,0,3:T(4,128)(4,1)S(1)} %compare_bitcast_fusion.5), kind=kOutput, calls=%fused_computation.34.clone.1 | convolution fusion | flops 78643200 | bytes 5571520 | tf_op jit(solution)/shard_map/while/body/eval_jaxpr/itr,rmc->itmc/dot_general | solution.py:66
  253.0 2.4 reshape.237
  255.4 6.7 %fusion.109 = f32[16,16,512]{2,1,0:T(8,128)S(1)} fusion(f32[8,512]{1,0:T(8,128)S(1)} %bitcast.114, bf16[16,3,80,512]{3,0,2,1:T(8,128)(2,1)} %fusion.107, bf16[8,16,3,16,80]{4,3,2,1,0:T(8,128)(2,1)S(1)} %reshape.237), kind=kOutput, calls=%fused_computation.30.clone.1 | convolution fusion | flops 505282560 | bytes 5455872 | tf_op jit(solution)/shard_map/while/body/eval_jaxpr/kitjm,itmc->kijc/dot_general | solution.py:69
  266.0 3.6 %fusion.107 = bf16[16,3,80,512]{3,0,2,1:T(8,128)(2,1)} fusion(bf16[20,80,512,1]{2,1,0,3:T(8,128)(2,1)S(1)} %dynamic-slice_bitcast_fusion.5, pred[16,3,20,1]{2,1,0,3:T(4,128)(4,1)S(1)} %compare_bitcast_fusion.5), kind=kOutput, calls=%fused_computation.34.clone.1 | convolution fusion | flops 78643200 | bytes 5571520 | tf_op jit(solution)/shard_map/while/body/eval_jaxpr/itr,rmc->itmc/dot_general | solution.py:66
  270.3 2.4 reshape.237
  272.8 6.7 %fusion.109 = f32[16,16,512]{2,1,0:T(8,128)S(1)} fusion(f32[8,512]{1,0:T(8,128)S(1)} %bitcast.114, bf16[16,3,80,512]{3,0,2,1:T(8,128)(2,1)} %fusion.107, bf16[8,16,3,16,80]{4,3,2,1,0:T(8,128)(2,1)S(1)} %reshape.237), kind=kOutput, calls=%fused_computation.30.clone.1 | convolution fusion | flops 505282560 | bytes 5455872 | tf_op jit(solution)/shard_map/while/body/eval_jaxpr/kitjm,itmc->kijc/dot_general | solution.py:69
  283.4 3.6 %fusion.107 = bf16[16,3,80,512]{3,0,2,1:T(8,128)(2,1)} fusion(bf16[20,80,512,1]{2,1,0,3:T(8,128)(2,1)S(1)} %dynamic-slice_bitcast_fusion.5, pred[16,3,20,1]{2,1,0,3:T(4,128)(4,1)S(1)} %compare_bitcast_fusion.5), kind=kOutput, calls=%fused_computation.34.clone.1 | convolution fusion | flops 78643200 | bytes 5571520 | tf_op jit(solution)/shard_map/while/body/eval_jaxpr/itr,rmc->itmc/dot_general | solution.py:66
  290.2 6.7 %fusion.109 = f32[16,16,512]{2,1,0:T(8,128)S(1)} fusion(f32[8,512]{1,0:T(8,128)S(1)} %bitcast.114, bf16[16,3,80,512]{3,0,2,1:T(8,128)(2,1)} %fusion.107, bf16[8,16,3,16,80]{4,3,2,1,0:T(8,128)(2,1)S(1)} %reshape.237), kind=kOutput, calls=%fused_computation.30.clone.1 | convolution fusion | flops 505282560 | bytes 5455872 | tf_op jit(solution)/shard_map/while/body/eval_jaxpr/kitjm,itmc->kijc/dot_general | solution.py:69
  (182 shorter events, 68.0 us)
Async XLA Ops:
  0.0 10.2 %copy-start.10 = (f32[2,1024]{1,0:T(2,128)S(1)}, f32[2,1024]{1,0:T(2,128)}, u32[]{:S(2)}) copy-start(f32[2,1024]{1,0:T(2,128)} %param.20) | copy-start | bytes 24580
  0.0 10.2 %copy-start.9 = (f32[2,8,512]{2,1,0:T(8,128)S(1)}, f32[2,8,512]{2,1,0:T(8,128)}, u32[]{:S(2)}) copy-start(f32[2,8,512]{2,1,0:T(8,128)} %param.17) | copy-start | bytes 98308
  0.0 60.6 %collective-permute-start = (bf16[64,16,512]{2,1,0:T(8,128)(2,1)}, bf16[64,16,512]{2,1,0:T(8,128)(2,1)}, u32[]{:S(2)}, u32[]{:S(2)}) collective-permute-start(bf16[64,16,512]{2,1,0:T(8,128)(2,1)} %param.13), channel_id=1, source_target_pairs={{14,0},{15,1},{0,2},{1,3},{2,4},{3,5},{4,6},{5,7},{6,8},{7,9},{8,1... | collective-permute-start | bytes 3145736 | tf_op jit(solution)/shard_map/ppermute | solution.py:10
  3.0 58.9 %collective-permute-start.1 = (bf16[64,16,512]{2,1,0:T(8,128)(2,1)}, bf16[64,16,512]{2,1,0:T(8,128)(2,1)}, u32[]{:S(2)}, u32[]{:S(2)}) collective-permute-start(bf16[64,16,512]{2,1,0:T(8,128)(2,1)} %param.13), channel_id=1, source_target_pairs={{15,0},{0,1},{1,2},{2,3},{3,4},{4,5},{5,6},{6,7},{7,8},{8,9},{9,10... | collective-permute-start | bytes 3145736 | tf_op jit(solution)/shard_map/ppermute | solution.py:10
  3.0 60.3 %collective-permute-start.2 = (bf16[64,16,512]{2,1,0:T(8,128)(2,1)}, bf16[64,16,512]{2,1,0:T(8,128)(2,1)S(1)}, u32[]{:S(2)}, u32[]{:S(2)}) collective-permute-start(bf16[64,16,512]{2,1,0:T(8,128)(2,1)} %param.13), channel_id=1, source_target_pairs={{1,0},{2,1},{3,2},{4,3},{5,4},{6,5},{7,6},{8,7},{9,8},{10,9},{11,1... | collective-permute-start | bytes 3145736 | tf_op jit(solution)/shard_map/ppermute | solution.py:10
  7.4 66.9 %collective-permute-start.3 = (bf16[64,16,512]{2,1,0:T(8,128)(2,1)}, bf16[64,16,512]{2,1,0:T(8,128)(2,1)S(1)}, u32[]{:S(2)}, u32[]{:S(2)}) collective-permute-start(bf16[64,16,512]{2,1,0:T(8,128)(2,1)} %param.13), channel_id=1, source_target_pairs={{2,0},{3,1},{4,2},{5,3},{6,4},{7,5},{8,6},{9,7},{10,8},{11,9},{12,... | collective-permute-start | bytes 3145736 | tf_op jit(solution)/shard_map/ppermute | solution.py:10
  10.2 52.9 %copy-start.4 = (bf16[64,16,512]{2,1,0:T(8,128)(2,1)S(1)}, bf16[64,16,512]{2,1,0:T(8,128)(2,1)}, u32[]{:S(2)}) copy-start(bf16[64,16,512]{2,1,0:T(8,128)(2,1)} %param.13) | copy-start | bytes 3145732
  63.3 14.0 %copy-start.8 = (s32[64,3]{0,1:T(4,128)S(1)}, s32[64,3]{0,1:T(4,128)}, u32[]{:S(2)}) copy-start(s32[64,3]{0,1:T(4,128)} %param.15) | copy-start | bytes 2308
  63.4 14.0 %copy-start.15 = (s32[64]{0:T(128)S(1)}, s32[64]{0:T(128)}, u32[]{:S(2)}) copy-start(s32[64]{0:T(128)} %param.14) | copy-start | bytes 772
  74.4 3.0 copy-start.2
  146.9 2.2 copy-start
  149.5 1.6 copy-start.11
  151.1 2.1 copy-start.5
  151.1 2.1 copy-start.13
  154.4 60.3 %copy-start.6 = (bf16[64,16,512]{2,1,0:T(8,128)(2,1)}, bf16[64,16,512]{2,1,0:T(8,128)(2,1)S(1)}, u32[]{:S(2)}) copy-start(bf16[64,16,512]{2,1,0:T(8,128)(2,1)S(1)} %add_convert_fusion.1) | copy-start | bytes 3145732
  154.4 57.7 %collective-permute-start.4 = (bf16[64,16,512]{2,1,0:T(8,128)(2,1)S(1)}, bf16[64,16,512]{2,1,0:T(8,128)(2,1)}, u32[]{:S(2)}, u32[]{:S(2)}) collective-permute-start(bf16[64,16,512]{2,1,0:T(8,128)(2,1)S(1)} %add_convert_fusion.1), channel_id=1, source_target_pairs={{14,0},{15,1},{0,2},{1,3},{2,4},{3,5},{4,6},{5,7},{6,8},{7,9},{8,1... | collective-permute-start | bytes 3145736 | tf_op jit(solution)/shard_map/ppermute | solution.py:10
  154.8 58.6 %collective-permute-start.5 = (bf16[64,16,512]{2,1,0:T(8,128)(2,1)S(1)}, bf16[64,16,512]{2,1,0:T(8,128)(2,1)}, u32[]{:S(2)}, u32[]{:S(2)}) collective-permute-start(bf16[64,16,512]{2,1,0:T(8,128)(2,1)S(1)} %add_convert_fusion.1), channel_id=1, source_target_pairs={{15,0},{0,1},{1,2},{2,3},{3,4},{4,5},{5,6},{6,7},{7,8},{8,9},{9,10... | collective-permute-start | bytes 3145736 | tf_op jit(solution)/shard_map/ppermute | solution.py:10
  154.8 60.0 %collective-permute-start.6 = (bf16[64,16,512]{2,1,0:T(8,128)(2,1)S(1)}, bf16[64,16,512]{2,1,0:T(8,128)(2,1)}, u32[]{:S(2)}, u32[]{:S(2)}) collective-permute-start(bf16[64,16,512]{2,1,0:T(8,128)(2,1)S(1)} %add_convert_fusion.1), channel_id=1, source_target_pairs={{1,0},{2,1},{3,2},{4,3},{5,4},{6,5},{7,6},{8,7},{9,8},{10,9},{11,1... | collective-permute-start | bytes 3145736 | tf_op jit(solution)/shard_map/ppermute | solution.py:10
  159.3 65.9 %collective-permute-start.7 = (bf16[64,16,512]{2,1,0:T(8,128)(2,1)S(1)}, bf16[64,16,512]{2,1,0:T(8,128)(2,1)S(1)}, u32[]{:S(2)}, u32[]{:S(2)}) collective-permute-start(bf16[64,16,512]{2,1,0:T(8,128)(2,1)S(1)} %add_convert_fusion.1), channel_id=1, source_target_pairs={{2,0},{3,1},{4,2},{5,3},{6,4},{7,5},{8,6},{9,7},{10,8},{11,9},{12,... | collective-permute-start | bytes 3145736 | tf_op jit(solution)/shard_map/ppermute | solution.py:10
  225.2 3.0 copy-start.3
  297.7 2.2 copy-start.1
  300.3 1.6 copy-start.12
  301.9 2.1 copy-start.7
  301.9 2.1 copy-start.14
where the time goes:
time: 307 us; the launch traced here: 306 us
  waiting for transfers between devices  121 us (39%)
  matrix products  93 us (30%)
  local copies, waits for them, and re-layouts  64.4 us (21%)
  starting transfers between devices  14.3 us (5%)
  other arithmetic  7.37 us (2%)
  loops' own time  5.68 us (2%)
    ppermute x8, waiting for transfers between devices, shifted(): return lax.ppermute(block, axis, route)  121 us
    dot_general x8, matrix products, one_block(): jnp.einsum('kitjm,itmc->kijc', banded, picked, preferred_element_type=jnp...  53.4 us
    dot_general x8, matrix products, one_block(): jnp.einsum('itr,rmc->itmc', selector, window, preferred_element_type=jnp....  28.8 us
    reshape x8, local copies, waits for them, and re-layouts, one_block(): banded.astype(jnp.bfloat16)  19.5 us
    ppermute x8, starting transfers between devices, shifted(): return lax.ppermute(block, axis, route)  14.3 us
    unnamed x42, local copies, waits for them, and re-layouts  12.6 us
    dynamic_slice x8, local copies, waits for them, and re-layouts, one_block(): lax.dynamic_slice_in_dim(widened, window_start, window_rows, axis=0)  12.3 us
    dynamic_update_slice x8, local copies, waits for them, and re-layouts, disco_strip(): filtered = lax.map(one_block, jnp.arange(blocks, dtype=jnp.int32))  6.8 us
  transfers between devices with their start and end apart: 8, of which 4 were waited for; matrix products, arithmetic and copies ran while one was open for 3% of the time, Pallas kernels for 0%

commit v1 on v0

v1 whole, which is shorter than its diff:
```python
import functools

import jax
import jax.numpy as jnp
import numpy as np
from jax import lax
from jax.experimental import pallas as pl
from jax.experimental.pallas import tpu as pltpu
from jax.sharding import PartitionSpec as P

TILE = 256


def block_kernel(
    far, idx_ref, band_ref, *refs
):
    if far:
        (self_ref, outer_ref, inner_ref, outer_far_ref, inner_far_ref), refs = refs[:5], refs[5:]
    else:
        (self_ref, outer_ref, inner_ref), refs = refs[:3], refs[3:]
    mix_ref, gain_ref, win_ref, bin_ref, wout_ref, out_ref, filtered, held = refs
    rows, cells, channels = out_ref.shape
    first = pl.program_id(0) * rows
    basis = mix_ref.shape[0]
    depth = (15 if far else 9) * cells

    def one_row(i, carry):
        at = (first + i) * 12
        pieces = []
        taps = [[idx_ref[at + 3 * kind + t] for t in range(3)] for kind in range(3)]
        for ref in (outer_ref, self_ref, inner_ref):
            kind = 0 if ref is self_ref else 1
            pieces += [ref[taps[kind][t]] for t in range(3)]
        if far:
            for ref in (outer_far_ref, inner_far_ref):
                pieces += [ref[taps[2][t]] for t in range(3)]
        picked = jnp.concatenate(pieces, axis=0)
        terms = jnp.dot(band_ref[i, :, :depth], picked, preferred_element_type=jnp.float32)
        total = terms[:cells] * mix_ref[0:1, :]
        for k in range(1, basis):
            total = total + terms[k * cells:(k + 1) * cells] * mix_ref[k:k + 1, :]
        place = pl.ds(pl.multiple_of(i * cells, cells), cells)
        filtered[place, :] = total
        held[place, :] = self_ref[idx_ref[at + 9]]
        return carry

    lax.fori_loop(0, rows, one_row, 0, unroll=2)
    value = filtered[...]
    centred = value - jnp.mean(value, axis=-1, keepdims=True)
    var = jnp.mean(centred * centred, axis=-1, keepdims=True)
    normed = (centred * lax.rsqrt(var + 1e-05) * gain_ref[...]).astype(jnp.bfloat16)
    pre = jnp.dot(normed, win_ref[...], preferred_element_type=jnp.float32) + bin_ref[...]
    hidden = jax.nn.gelu(pre, approximate=True).astype(jnp.bfloat16)
    update = jnp.dot(hidden, wout_ref[...], preferred_element_type=jnp.float32)
    out = (held[...].astype(jnp.float32) + update).astype(jnp.bfloat16)
    out_ref[...] = out.reshape(rows, cells, channels)


def run_block(idx, band, fields, weights, far, blocks):
    mix, gain, win, bias, wout = weights
    total_rows = band.shape[0]
    rows = total_rows // blocks
    cells, channels = fields[0].shape[1:]
    whole = lambda a: pl.BlockSpec(a.shape, lambda g, s, n=a.ndim: (0,) * n)
    tail = list(fields) + [mix, gain, win, bias, wout]
    grid = pltpu.PrefetchScalarGridSpec(
        num_scalar_prefetch=1,
        grid=(blocks,),
        in_specs=[pl.BlockSpec((rows,) + band.shape[1:], lambda g, s: (g, 0, 0))]
        + [whole(a) for a in tail],
        out_specs=pl.BlockSpec((rows, cells, channels), lambda g, s: (g, 0, 0)),
        scratch_shapes=[
            pltpu.VMEM((rows * cells, channels), jnp.float32),
            pltpu.VMEM((rows * cells, channels), jnp.bfloat16),
        ],
    )
    flops = total_rows * cells * channels * (2 * 8 * 240 + 4 * win.shape[1])
    return pl.pallas_call(
        functools.partial(block_kernel, far),
        out_shape=jax.ShapeDtypeStruct((total_rows, cells, channels), jnp.bfloat16),
        grid_spec=grid,
        cost_estimate=pl.CostEstimate(
            flops=flops, bytes_accessed=16 * 2**20, transcendentals=total_rows * cells * 1024
        ),
        compiler_params=pltpu.CompilerParams(vmem_limit_bytes=44 * 2**20),
    )(idx, band, *tail)


def banded(filter_set, zonal_width, cells, sign):
    basis, lat, taps, offsets = filter_set.shape
    half = (offsets - 1) // 2
    d = jnp.arange(offsets, dtype=jnp.int32)
    support = jnp.abs(d - half)[None, :] <= zonal_width[:, None]
    masked = jnp.where(support[None, :, None, :], filter_set, jnp.zeros((), filter_set.dtype))
    masked = masked.transpose(1, 0, 2, 3).reshape(lat * basis, taps * offsets)
    col = jnp.arange(TILE, dtype=jnp.int32)
    piece, tap, m = col // (taps * cells), (col // cells) % taps, col % cells
    place = jnp.array([-1, 0, 1, -2, 2, 99], jnp.int32)[jnp.minimum(piece, 5)] * sign
    j = jnp.arange(cells, dtype=jnp.int32)
    want = place[None, :] * cells + m[None, :] - j[:, None] + half
    table = (
        (want[None, None] == d[None, :, None, None])
        & (tap[None, None, None, :] == jnp.arange(taps)[:, None, None, None])
    )
    table = table.astype(jnp.bfloat16).reshape(taps * offsets, cells * TILE)
    band = jnp.dot(masked, table, preferred_element_type=jnp.float32).astype(jnp.bfloat16)
    return band.reshape(lat, basis * cells, TILE)


def packed(rows, top, bottom, lat):
    return jnp.where(
        rows < top, rows, jnp.where(rows >= bottom, rows - bottom + top, rows + lat - bottom)
    )


def per_device(
    state, zonal_width, tap_rows, filters, basis_mix, norm_gain, weight_in, bias_in, weight_out
):
    lat, cells, channels = state.shape
    devices = lax.axis_size("lon")
    me = lax.axis_index("lon")
    sign = 1 - 2 * (me % 2)
    n = devices
    to_outer = [(i, (i - 1) % n if i % 2 == 0 else (i + 1) % n) for i in range(n)]
    to_inner = [(i, i ^ 1) for i in range(n)]
    to_far = [(i, (i + 2) % n if i % 2 == 0 else (i - 2) % n) for i in range(n)]
    send = lambda x, route: lax.ppermute(x, "lon", route)
    q = lat // 4
    ends = lambda x, a: jnp.concatenate([x[:a], x[lat - a:]], axis=0)

    def indices(rows, self_at, near_at, far_top):
        taps = tap_rows[rows]
        far_at = packed(taps, far_top, lat - far_top, lat)
        far_at = jnp.clip(far_at, 0, 2 * far_top - 1)
        own = self_at(jnp.asarray(rows, jnp.int32))[:, None]
        pad = jnp.zeros((len(rows), 2), jnp.int32)
        return jnp.concatenate([self_at(taps), near_at(taps), far_at, own, pad], axis=1).reshape(-1)

    def weights(l):
        return (
            basis_mix[l], norm_gain[l][None], weight_in[l], bias_in[l][None], weight_out[l]
        )


    same = lambda r: r
    a, b = q + 4, q + 2
    at_a = lambda r: packed(r, a, lat - a, lat)
    at_b = lambda r: packed(r, b, lat - b, lat)

    rows_p = np.concatenate([np.arange(b), np.arange(lat - b, lat)])
    rows_m = np.arange(b, lat - b)
    outer_p = send(ends(state, a), to_outer)
    far_out = send(ends(state, b), to_far)
    inner = send(jnp.concatenate([state[:a], state[lat - a:], state[a:lat - a]], axis=0), to_inner)
    late, outer_p = lax.optimization_barrier((state[a:lat - a], outer_p))
    far_in = send(jnp.concatenate([outer_p[:b], outer_p[2 * a - b:]], axis=0), to_inner)
    outer_m = send(late, to_outer)
    band1 = banded(filters[0], zonal_width, cells, sign)
    band2 = banded(filters[1], zonal_width, cells, sign)
    new_p = run_block(
        indices(rows_p, same, at_a, b), jnp.concatenate([band1[:b], band1[lat - b:]]),
        (state, outer_p, inner, far_out, far_in), weights(0), True, 2,
    )
    outer2_p = send(new_p, to_outer)
    far2_out = send(new_p, to_far)
    inner2_p = send(new_p, to_inner)
    new_m = run_block(
        indices(rows_m, same, at_a, b), band1[b:lat - b],
        (state, jnp.concatenate([outer_p, outer_m], axis=0), inner), weights(0), False, 2,
    )
    far2_in = send(outer2_p, to_inner)
    late2, outer2_p = lax.optimization_barrier((new_m, outer2_p))
    outer2_m = send(late2, to_outer)
    inner2_m = send(new_m, to_inner)
    rows_p2 = np.concatenate([np.arange(q), np.arange(lat - q, lat)])
    rows_m2 = np.arange(q, lat - q)
    out_p = run_block(
        indices(rows_p2, at_b, at_b, b), jnp.concatenate([band2[:q], band2[lat - q:]]),
        (new_p, outer2_p, inner2_p, far2_out, far2_in), weights(1), True, 2,
    )
    out_m = run_block(
        indices(rows_m2, at_b, at_b, b), band2[q:lat - q],
        (
            jnp.concatenate([new_p, new_m], axis=0),
            jnp.concatenate([outer2_p, outer2_m], axis=0),
            jnp.concatenate([inner2_p, inner2_m], axis=0),
        ), weights(1), False, 2,
    )
    return jnp.concatenate([out_p[:q], out_m, out_p[q:]], axis=0)


def solution(mesh):
    placed = (P("parts", "lon", None), P(), P(), P(), P(), P(), P(), P(), P())
    return jax.shard_map(
        per_device, mesh=mesh, in_specs=placed, out_specs=P("parts", "lon", None), check_vma=False
    )
```

time: 307 us -> 108 us (0.35)
  waiting for transfers between devices: 121 us -> 1.72 us
  matrix products: 93 us -> 3.69 us
  Pallas kernels: 0 us -> 31.4 us
  local copies, waits for them, and re-layouts: 64.4 us -> 40.3 us
  other arithmetic: 7.37 us -> 14 us
  loops' own time: 5.68 us -> 0 us
    ppermute x8 -> x11, waiting for transfers between devices: 121 us -> 1.72 us  [per_device(): send = lambda x, route: lax.ppermute(x, 'lon', route)]
    dot_general x28 -> x2, matrix products: 93 us -> 3.69 us  [banded(): jnp.dot(masked, table, preferred_element_type=jnp.float32)]
    pallas_call x0 -> x4, Pallas kernels: none -> 31.4 us  [run_block(): pl.pallas_call(functools.partial(block_kernel, far), out_shape=jax.ShapeD...]
    slice x4 -> x17, local copies, waits for them, and re-layouts: 1.95 us -> 25.9 us  [the longest x2 6.87 us: per_device(): band1[b:lat - b]]
    dynamic_slice x40 -> x0, local copies, waits for them, and re-layouts: 19.1 us -> none  [the longest x8 12.3 us: one_block(): lax.dynamic_slice_in_dim(widened, window_start, window_rows, axis=0)]
    reshape x16 -> x6, local copies, waits for them, and re-layouts: 20.1 us -> 2.13 us  [the longest x2 1.69 us: banded(): masked = masked.transpose(1, 0, 2, 3).reshape(lat * basis, taps * offsets)]
    concatenate x0 -> x11, other arithmetic: none -> 12.4 us  [the longest x1 2.08 us: per_device(): jnp.concatenate([state[:a], state[lat - a:], state[a:lat - a]], axis=0)]
    unnamed x42 -> x59, local copies, waits for them, and re-layouts: 12.6 us -> 4.78 us
  transfers between devices with their start and end apart: 8 -> 11, of which waited for: 4 -> 1; matrix products, arithmetic and copies ran while one was open for 3% -> 48% of each run, Pallas kernels for 0% -> 22%
where the time goes in v1:
time: 108 us; the launch traced here: 107 us
  local copies, waits for them, and re-layouts  40.3 us (37%)
  Pallas kernels  31.4 us (29%)
  starting transfers between devices  15.4 us (14%)
  other arithmetic  14 us (13%)
  matrix products  3.69 us (3%)
  waiting for transfers between devices  1.72 us (2%)
    pallas_call x4, Pallas kernels, run_block(): pl.pallas_call(functools.partial(block_kernel, far), out_shape=jax.ShapeD...  31.4 us
    ppermute x11, starting transfers between devices, per_device(): send = lambda x, route: lax.ppermute(x, 'lon', route)  15.4 us
    slice x2, local copies, waits for them, and re-layouts, per_device(): band1[b:lat - b]  6.87 us
    unnamed x59, local copies, waits for them, and re-layouts  4.78 us
    slice x2, local copies, waits for them, and re-layouts, per_device(): band2[q:lat - q]  4.45 us
    slice x2, local copies, waits for them, and re-layouts, per_device(): band1[:b]  4.17 us
    slice x2, local copies, waits for them, and re-layouts, per_device(): band2[:q]  3.95 us
    dot_general x2, matrix products, banded(): jnp.dot(masked, table, preferred_element_type=jnp.float32)  3.69 us
  transfers between devices with their start and end apart: 11, of which 1 were waited for; matrix products, arithmetic and copies ran while one was open for 48% of the time, Pallas kernels for 22%

profile of v1, /device:TPU:0, one launch (start us, length us, event | category | flops | bytes accessed | tf_op | source)
XLA Modules:
  0.0 107.0 jit_solution(12340221591168286667)
XLA Ops:
  0.0 1.2 %fusion.12 = (bf16[20,16,512]{2,1,0:T(8,128)(2,1)S(1)}, bf16[20,16,512]{2,1,0:T(8,128)(2,1)S(1)}) fusion(bf16[64,16,512]{2,1,0:T(8,128)(2,1)} %refs_0_.3), kind=kLoop, calls=%fused_computation.71 | loop fusion | bytes 1310720 | tf_op jit(solution)/shard_map/slice | solution.py:129
  2.1 5.4 %collective-permute-start = (bf16[40,16,512]{2,1,0:T(8,128)(2,1)}, bf16[40,16,512]{2,1,0:T(8,128)(2,1)S(1)}, u32[]{:S(2)}, u32[]{:S(2)}) collective-permute-start(bf16[40,16,512]{2,1,0:T(8,128)(2,1)} %pad_maximum_fusion.8), channel_id=1, source_target_pairs={{0,15},{1,2},{2,1},{3,4},{4,3},{5,6},{6,5},{7,8},{8,7},{9,10},{10,... | collective-permute-start | bytes 1966088 | tf_op jit(solution)/shard_map/ppermute | solution.py:127
  8.4 2.1 %pad_maximum_fusion.2 = bf16[64,16,512]{2,1,0:T(8,128)(2,1)} fusion(bf16[24,16,512]{2,1,0:T(8,128)(2,1)} %slice.122, bf16[20,16,512]{2,1,0:T(8,128)(2,1)S(1)} %get-tuple-element.24, bf16[20,16,512]{2,1,0:T(8,128)(2,1)S(1)} %get-tuple-element.23), kind=kLoop, calls=%fused_computation.10 | loop fusion | flops 1048576 | bytes 2097152 | tf_op jit(solution)/shard_map/concatenate | solution.py:154
  14.5 1.3 %convolution_convert_fusion = bf16[512,4096]{1,0:T(8,128)(2,1)S(1)} fusion(bf16[512,195]{1,0:T(8,128)(2,1)S(1)} %reshape.254, pred[195,4096]{1,0:T(8,128)(4,1)S(1)} %bitcast.35), kind=kOutput, calls=%fused_computation.4 | convolution fusion | flops 819986432 | bytes 5192704 | tf_op jit(solution)/shard_map/dot_general | solution.py:106
  15.8 1.7 %fusion.9 = (bf16[144,4096]{1,0:T(8,128)(2,1)}, bf16[144,4096]{1,0:T(8,128)(2,1)}) fusion(bf16[512,4096]{1,0:T(8,128)(2,1)S(1)} %convolution_convert_fusion), kind=kLoop, calls=%fused_computation.68 | loop fusion | bytes 4718592 | tf_op jit(solution)/shard_map/slice | solution.py:161
  18.5 2.5 %slice.119 = bf16[18,128,256]{2,1,0:T(8,128)(2,1)S(1)} reshape(bf16[144,4096]{1,0:T(8,128)(2,1)} %get-tuple-element.13) | data formatting | bytes 2359296 | tf_op jit(solution)/shard_map/slice | solution.py:161
  21.0 3.1 %slice.121 = bf16[18,128,256]{2,1,0:T(8,128)(2,1)} reshape(bf16[144,4096]{1,0:T(8,128)(2,1)} %get-tuple-element.14) | data formatting | bytes 2359296 | tf_op jit(solution)/shard_map/slice | solution.py:161
  25.7 2.2 %copy.45 = bf16[64,8,3,65]{3,2,1,0:T(4,128)(2,1)} copy(bf16[64,8,3,65]{3,0,2,1:T(8,128)(2,1)} %get-tuple-element.26) | data formatting | bytes 399360 | tf_op jit(solution)/shard_map/transpose | solution.py:95
  27.8 1.4 %reshape.252 = bf16[512,195]{1,0:T(8,128)(2,1)S(1)} reshape(bf16[64,8,3,65]{3,2,1,0:T(4,128)(2,1)} %copy.45) | data formatting | bytes 399360 | tf_op jit(solution)/shard_map/reshape | solution.py:95
  29.3 2.4 %convolution_convert_fusion.1 = bf16[512,4096]{1,0:T(8,128)(2,1)S(1)} fusion(bf16[512,195]{1,0:T(8,128)(2,1)S(1)} %reshape.252, pred[195,4096]{1,0:T(8,128)(4,1)} %bitcast.36), kind=kOutput, calls=%fused_computation.5 | convolution fusion | flops 819986432 | bytes 5192704 | tf_op jit(solution)/shard_map/dot_general | solution.py:106
  31.7 1.5 %fusion.10 = (bf16[128,4096]{1,0:T(8,128)(2,1)}, bf16[128,4096]{1,0:T(8,128)(2,1)}) fusion(bf16[512,4096]{1,0:T(8,128)(2,1)S(1)} %convolution_convert_fusion.1), kind=kLoop, calls=%fused_computation.69 | loop fusion | bytes 4194304 | tf_op jit(solution)/shard_map/slice | solution.py:178
  36.9 1.1 %slice_bitcast_fusion = (bf16[1024,512]{1,0:T(8,128)(2,1)}, bf16[1024,512]{1,0:T(8,128)(2,1)S(1)}) fusion(bf16[2,1024,512]{2,1,0:T(8,128)(2,1)S(1)} %copy-done.11), kind=kLoop, calls=%fused_computation.16 | loop fusion | bytes 4194304 | tf_op jit(solution)/shard_map/squeeze | solution.py:141
  38.0 1.2 %slice_bitcast_fusion.1 = (bf16[512,1024]{1,0:T(8,128)(2,1)}, bf16[512,1024]{1,0:T(8,128)(2,1)S(1)}) fusion(bf16[2,512,1024]{2,1,0:T(8,128)(2,1)S(1)} %copy-done.12), kind=kLoop, calls=%fused_computation.17 | loop fusion | bytes 4194304 | tf_op jit(solution)/shard_map/squeeze | solution.py:141
  39.2 3.9 %collective-permute-start.4 = (bf16[24,16,512]{2,1,0:T(8,128)(2,1)}, bf16[24,16,512]{2,1,0:T(8,128)(2,1)}, u32[]{:S(2)}, u32[]{:S(2)}) collective-permute-start(bf16[24,16,512]{2,1,0:T(8,128)(2,1)} %slice.122), channel_id=1, source_target_pairs={{0,15},{1,2},{2,1},{3,4},{4,3},{5,6},{6,5},{7,8},{8,7},{9,10},{10,... | collective-permute-start | bytes 1179656 | tf_op jit(solution)/shard_map/ppermute | solution.py:127
  43.1 9.3 %shard_map.217.refs_0_ = bf16[36,16,512]{2,1,0:T(8,128)(2,1)} custom-call(s32[432]{0:T(512)S(1)} %reshape.253.idx_ref, bf16[36,128,256]{2,1,0:T(8,128)(2,1)S(1)} %pad_maximum_fusion.band_ref, bf16[64,16,512]{2,1,0:T(8,128)(2,1)S(1)} %copy-done, bf16[40,16,512]{2,1,0:T(8,128)(2,1)S(1)} %copy-done.3, bf16[64,16,512]{2,1,0:T(8,128)(2,1)} %collective-permute-done.1.refs_2_, ...), custom_call_target="tpu_custom_call" | custom-call | flops 2340421632 | bytes 16777216 | tf_op jit(solution)/shard_map/pallas_call | solution.py:78
  53.0 2.9 %slice.164 = bf16[224,4096]{1,0:T(8,128)(2,1)} slice(bf16[512,4096]{1,0:T(8,128)(2,1)} %copy-done.7), slice={[144:368], [0:4096]} | slice | bytes 3670016 | tf_op jit(solution)/shard_map/slice | solution.py:168
  55.9 3.9 %slice.135.band_ref = bf16[28,128,256]{2,1,0:T(8,128)(2,1)} reshape(bf16[224,4096]{1,0:T(8,128)(2,1)} %slice.164) | data formatting | bytes 3670016 | tf_op jit(solution)/shard_map/slice | solution.py:168
  61.2 1.4 %pad_maximum_fusion.3.refs_1_ = bf16[64,16,512]{2,1,0:T(8,128)(2,1)S(1)} fusion(bf16[24,16,512]{2,1,0:T(8,128)(2,1)} %collective-permute-done.4, bf16[40,16,512]{2,1,0:T(8,128)(2,1)} %copy-done.2), kind=kLoop, calls=%fused_computation.11 | loop fusion | flops 524288 | bytes 2097152 | tf_op jit(solution)/shard_map/concatenate | solution.py:169
  63.0 7.8 %shard_map.218 = bf16[28,16,512]{2,1,0:T(8,128)(2,1)} custom-call(s32[336]{0:T(512)S(1)} %reshape.255.idx_ref, bf16[28,128,256]{2,1,0:T(8,128)(2,1)S(1)} %copy-done.1, bf16[64,16,512]{2,1,0:T(8,128)(2,1)S(1)} %copy-done, bf16[64,16,512]{2,1,0:T(8,128)(2,1)S(1)} %pad_maximum_fusion.3.refs_1_, bf16[64,16,512]{2,1,0:T(8,128)(2,1)} %collective-permute-done.1.refs_2_, ...), custom_call_target="tpu_custom_call" | custom-call | flops 1820327936 | bytes 16777216 | tf_op jit(solution)/shard_map/pallas_call | solution.py:78
  70.8 3.9 %collective-permute-start.9 = (bf16[28,16,512]{2,1,0:T(8,128)(2,1)}, bf16[28,16,512]{2,1,0:T(8,128)(2,1)}, u32[]{:S(2)}, u32[]{:S(2)}) collective-permute-start(bf16[28,16,512]{2,1,0:T(8,128)(2,1)} %shard_map.218), channel_id=1, source_target_pairs={{0,15},{1,2},{2,1},{3,4},{4,3},{5,6},{6,5},{7,8},{8,7},{9,10},{10,... | collective-permute-start | bytes 1376264 | tf_op jit(solution)/shard_map/ppermute | solution.py:127
  74.7 1.6 %slice.166 = bf16[256,4096]{1,0:T(8,128)(2,1)} slice(bf16[512,4096]{1,0:T(8,128)(2,1)S(1)} %copy-done.9), slice={[128:384], [0:4096]} | slice | bytes 4194304 | tf_op jit(solution)/shard_map/slice | solution.py:182
  76.3 2.9 %slice.143.band_ref = bf16[32,128,256]{2,1,0:T(8,128)(2,1)S(1)} reshape(bf16[256,4096]{1,0:T(8,128)(2,1)} %slice.166) | data formatting | bytes 4194304 | tf_op jit(solution)/shard_map/slice | solution.py:182
  79.4 2.4 %slice.114 = bf16[16,128,256]{2,1,0:T(8,128)(2,1)} reshape(bf16[128,4096]{1,0:T(8,128)(2,1)} %get-tuple-element.15) | data formatting | bytes 2097152 | tf_op jit(solution)/shard_map/slice | solution.py:178
  81.8 1.3 %slice.116 = bf16[16,128,256]{2,1,0:T(8,128)(2,1)} reshape(bf16[128,4096]{1,0:T(8,128)(2,1)S(1)} %copy-done.10) | data formatting | bytes 2097152 | tf_op jit(solution)/shard_map/slice | solution.py:178
  83.3 1.7 %pad_maximum_fusion.1.band_ref = bf16[32,128,256]{2,1,0:T(8,128)(2,1)S(1)} fusion(bf16[16,128,256]{2,1,0:T(8,128)(2,1)} %slice.116, bf16[16,128,256]{2,1,0:T(8,128)(2,1)} %slice.114), kind=kLoop, calls=%fused_computation.7 | loop fusion | flops 1048576 | bytes 4194304 | tf_op jit(solution)/shard_map/concatenate | solution.py:178
  85.8 1.3 %pad_maximum_fusion.4.refs_0_ = bf16[64,16,512]{2,1,0:T(8,128)(2,1)S(1)} fusion(bf16[28,16,512]{2,1,0:T(8,128)(2,1)} %shard_map.218, bf16[36,16,512]{2,1,0:T(8,128)(2,1)} %shard_map.217.refs_0_), kind=kLoop, calls=%fused_computation.12 | loop fusion | flops 524288 | bytes 2097152 | tf_op jit(solution)/shard_map/concatenate | solution.py:184
  87.1 1.4 %pad_maximum_fusion.6.refs_2_ = bf16[64,16,512]{2,1,0:T(8,128)(2,1)S(1)} fusion(bf16[28,16,512]{2,1,0:T(8,128)(2,1)} %collective-permute-done.10, bf16[36,16,512]{2,1,0:T(8,128)(2,1)} %collective-permute-done.6.refs_2_), kind=kLoop, calls=%fused_computation.14 | loop fusion | flops 524288 | bytes 2097152 | tf_op jit(solution)/shard_map/concatenate | solution.py:186
  88.6 1.3 %pad_maximum_fusion.5.refs_1_ = bf16[64,16,512]{2,1,0:T(8,128)(2,1)S(1)} fusion(bf16[28,16,512]{2,1,0:T(8,128)(2,1)} %collective-permute-done.9, bf16[36,16,512]{2,1,0:T(8,128)(2,1)} %collective-permute-done.5.refs_1_), kind=kLoop, calls=%fused_computation.13 | loop fusion | flops 524288 | bytes 2097152 | tf_op jit(solution)/shard_map/concatenate | solution.py:185
  89.9 6.3 %shard_map.220 = bf16[32,16,512]{2,1,0:T(8,128)(2,1)S(1)} custom-call(s32[384]{0:T(512)S(1)} %reshape.256.idx_ref, bf16[32,128,256]{2,1,0:T(8,128)(2,1)S(1)} %slice.143.band_ref, bf16[64,16,512]{2,1,0:T(8,128)(2,1)S(1)} %pad_maximum_fusion.4.refs_0_, bf16[64,16,512]{2,1,0:T(8,128)(2,1)S(1)} %pad_maximum_fusion.5.refs_1_, ...), custom_call_target="tpu_custom_call" | custom-call | flops 2080374784 | bytes 16777216 | tf_op jit(solution)/shard_map/pallas_call | solution.py:78
  96.2 1.7 %collective-permute-done.7.refs_3_ = bf16[36,16,512]{2,1,0:T(8,128)(2,1)S(1)} collective-permute-done((bf16[36,16,512]{2,1,0:T(8,128)(2,1)}, bf16[36,16,512]{2,1,0:T(8,128)(2,1)S(1)}, u32[]{:S(2)}, u32[]{:S(2)}) %collective-permute-start.7) | collective-permute-done | bytes 589856 | tf_op jit(solution)/shard_map/ppermute | solution.py:127
  97.9 8.0 %shard_map.219 = bf16[32,16,512]{2,1,0:T(8,128)(2,1)S(1)} custom-call(s32[384]{0:T(512)S(1)} %reshape.251.idx_ref, bf16[32,128,256]{2,1,0:T(8,128)(2,1)S(1)} %pad_maximum_fusion.1.band_ref, bf16[36,16,512]{2,1,0:T(8,128)(2,1)} %shard_map.217.refs_0_, bf16[36,16,512]{2,1,0:T(8,128)(2,1)} %collective-permute-done.5.refs_1_, ...), custom_call_target="tpu_custom_call" | custom-call | flops 2080374784 | bytes 16777216 | tf_op jit(solution)/shard_map/pallas_call | solution.py:78
  105.9 1.1 %pad_maximum_fusion.7 = bf16[64,16,512]{2,1,0:T(8,128)(2,1)} fusion(bf16[16,16,512]{2,1,0:T(8,128)(2,1)S(1)} %get-tuple-element.30, bf16[32,16,512]{2,1,0:T(8,128)(2,1)S(1)} %shard_map.220, bf16[16,16,512]{2,1,0:T(8,128)(2,1)S(1)} %get-tuple-element.29), kind=kLoop, calls=%fused_computation.15 | loop fusion | flops 1048576 | bytes 2097152 | tf_op jit(solution)/shard_map/concatenate | solution.py:189
  (123 shorter events, 15.2 us)
Async XLA Ops:
  0.0 7.6 %copy-start = (bf16[64,16,512]{2,1,0:T(8,128)(2,1)S(1)}, bf16[64,16,512]{2,1,0:T(8,128)(2,1)}, u32[]{:S(2)}) copy-start(bf16[64,16,512]{2,1,0:T(8,128)(2,1)} %refs_0_.3) | copy-start | bytes 3145732
  2.1 33.0 %collective-permute-start = (bf16[40,16,512]{2,1,0:T(8,128)(2,1)}, bf16[40,16,512]{2,1,0:T(8,128)(2,1)S(1)}, u32[]{:S(2)}, u32[]{:S(2)}) collective-permute-start(bf16[40,16,512]{2,1,0:T(8,128)(2,1)} %pad_maximum_fusion.8), channel_id=1, source_target_pairs={{0,15},{1,2},{2,1},{3,4},{4,3},{5,6},{6,5},{7,8},{8,7},{9,10},{10,... | collective-permute-start | bytes 1966088 | tf_op jit(solution)/shard_map/ppermute | solution.py:127
  10.5 32.6 %collective-permute-start.1 = (bf16[64,16,512]{2,1,0:T(8,128)(2,1)}, bf16[64,16,512]{2,1,0:T(8,128)(2,1)}, u32[]{:S(2)}, u32[]{:S(2)}) collective-permute-start(bf16[64,16,512]{2,1,0:T(8,128)(2,1)} %pad_maximum_fusion.2), channel_id=1, source_target_pairs={{0,1},{1,0},{2,3},{3,2},{4,5},{5,4},{6,7},{7,6},{8,9},{9,8},{10,11... | collective-permute-start | bytes 3145736 | tf_op jit(solution)/shard_map/ppermute | solution.py:127
  11.4 31.7 %collective-permute-start.2 = (bf16[36,16,512]{2,1,0:T(8,128)(2,1)}, bf16[36,16,512]{2,1,0:T(8,128)(2,1)}, u32[]{:S(2)}, u32[]{:S(2)}) collective-permute-start(bf16[36,16,512]{2,1,0:T(8,128)(2,1)} %pad_maximum_fusion.9), channel_id=1, source_target_pairs={{0,2},{1,15},{2,4},{3,1},{4,6},{5,3},{6,8},{7,5},{8,10},{9,7},{10,... | collective-permute-start | bytes 1769480 | tf_op jit(solution)/shard_map/ppermute | solution.py:127
  12.9 2.9 %copy-start.13 = (pred[25,8,16,256]{3,1,2,0:T(8,128)(4,1)}, pred[25,8,16,256]{3,1,2,0:T(8,128)(4,1)S(1)}, u32[]{:S(2)}) copy-start(pred[25,8,16,256]{3,1,2,0:T(8,128)(4,1)S(1)} %copy.50) | copy-start | bytes 2457604
  15.8 2.7 %copy-start.7 = (bf16[512,4096]{1,0:T(8,128)(2,1)}, bf16[512,4096]{1,0:T(8,128)(2,1)S(1)}, u32[]{:S(2)}) copy-start(bf16[512,4096]{1,0:T(8,128)(2,1)S(1)} %convolution_convert_fusion) | copy-start | bytes 12582916
  18.5 5.6 %copy-start.22 = (s32[64,3]{0,1:T(4,128)S(1)}, s32[64,3]{0,1:T(4,128)}, u32[]{:S(2)}) copy-start(s32[64,3]{0,1:T(4,128)} %param.25) | copy-start | bytes 2308
  18.5 5.7 %copy-start.27 = (s32[36]{0:T(128)S(1)}, s32[36]{0:T(128)}, u32[]{:S(2)}) copy-start(s32[36]{0:T(128)} %constant.208) | copy-start | bytes 436
  18.5 6.3 %copy-start.16 = (s32[36,1]{1,0:T(8,128)S(1)}, s32[36,1]{1,0:T(8,128)}, u32[]{:S(2)}) copy-start(s32[36,1]{1,0:T(8,128)} %constant.177) | copy-start | bytes 436
  18.5 6.5 %copy-start.20 = (f32[2,1024]{1,0:T(2,128)S(1)}, f32[2,1024]{1,0:T(2,128)}, u32[]{:S(2)}) copy-start(f32[2,1024]{1,0:T(2,128)} %param.30) | copy-start | bytes 24580
  18.5 6.5 %copy-start.21 = (f32[2,512]{1,0:T(2,128)S(1)}, f32[2,512]{1,0:T(2,128)}, u32[]{:S(2)}) copy-start(f32[2,512]{1,0:T(2,128)} %param.28) | copy-start | bytes 12292
  18.5 6.6 %copy-start.26 = (s32[28]{0:T(128)S(1)}, s32[28]{0:T(128)}, u32[]{:S(2)}) copy-start(s32[28]{0:T(128)} %constant.209) | copy-start | bytes 340
  31.7 2.6 %copy-start.8 = (bf16[512,4096]{1,0:T(8,128)(2,1)}, bf16[512,4096]{1,0:T(8,128)(2,1)S(1)}, u32[]{:S(2)}) copy-start(bf16[512,4096]{1,0:T(8,128)(2,1)S(1)} %convolution_convert_fusion.1) | copy-start | bytes 12582916
  31.7 2.6 %copy-start.6 = (bf16[18,128,256]{2,1,0:T(8,128)(2,1)S(1)}, bf16[18,128,256]{2,1,0:T(8,128)(2,1)}, u32[]{:S(2)}) copy-start(bf16[18,128,256]{2,1,0:T(8,128)(2,1)} %slice.121) | copy-start | bytes 3538948
  36.0 2.0 %copy-start.12 = (bf16[2,512,1024]{2,1,0:T(8,128)(2,1)S(1)}, bf16[2,512,1024]{2,1,0:T(8,128)(2,1)}, u32[]{:S(2)}) copy-start(bf16[2,512,1024]{2,1,0:T(8,128)(2,1)} %param.29) | copy-start | bytes 6291460
  36.0 7.1 %collective-permute-start.3 = (bf16[36,16,512]{2,1,0:T(8,128)(2,1)S(1)}, bf16[36,16,512]{2,1,0:T(8,128)(2,1)S(1)}, u32[]{:S(2)}, u32[]{:S(2)}) collective-permute-start(bf16[36,16,512]{2,1,0:T(8,128)(2,1)S(1)} %pad_maximum_fusion.10), channel_id=1, source_target_pairs={{0,1},{1,0},{2,3},{3,2},{4,5},{5,4},{6,7},{7,6},{8,9},{9,8},{10,11... | collective-permute-start | bytes 1769480 | tf_op jit(solution)/shard_map/ppermute | solution.py:127
  38.0 5.1 %copy-start.3 = (bf16[40,16,512]{2,1,0:T(8,128)(2,1)S(1)}, bf16[40,16,512]{2,1,0:T(8,128)(2,1)}, u32[]{:S(2)}) copy-start(bf16[40,16,512]{2,1,0:T(8,128)(2,1)} %copy-done.2) | copy-start | bytes 1966084
  39.2 22.0 %collective-permute-start.4 = (bf16[24,16,512]{2,1,0:T(8,128)(2,1)}, bf16[24,16,512]{2,1,0:T(8,128)(2,1)}, u32[]{:S(2)}, u32[]{:S(2)}) collective-permute-start(bf16[24,16,512]{2,1,0:T(8,128)(2,1)} %slice.122), channel_id=1, source_target_pairs={{0,15},{1,2},{2,1},{3,4},{4,3},{5,6},{6,5},{7,8},{8,7},{9,10},{10,... | collective-permute-start | bytes 1179656 | tf_op jit(solution)/shard_map/ppermute | solution.py:127
  43.1 9.8 %copy-start.24 = (s32[32]{0:T(128)S(1)}, s32[32]{0:T(128)}, u32[]{:S(2)}) copy-start(s32[32]{0:T(128)} %constant.193) | copy-start | bytes 388
  52.4 18.4 %collective-permute-start.5 = (bf16[36,16,512]{2,1,0:T(8,128)(2,1)}, bf16[36,16,512]{2,1,0:T(8,128)(2,1)}, u32[]{:S(2)}, u32[]{:S(2)}) collective-permute-start(bf16[36,16,512]{2,1,0:T(8,128)(2,1)} %shard_map.217.refs_0_), channel_id=1, source_target_pairs={{0,15},{1,2},{2,1},{3,4},{4,3},{5,6},{6,5},{7,8},{8,7},{9,10},{10,... | collective-permute-start | bytes 1769480 | tf_op jit(solution)/shard_map/ppermute | solution.py:127
  55.9 3.9 %copy-start.19 = (s32[28,1]{1,0:T(8,128)S(1)}, s32[28,1]{1,0:T(8,128)}, u32[]{:S(2)}) copy-start(s32[28,1]{1,0:T(8,128)} %constant.178) | copy-start | bytes 340
  62.6 12.1 %copy-start.9 = (bf16[512,4096]{1,0:T(8,128)(2,1)S(1)}, bf16[512,4096]{1,0:T(8,128)(2,1)}, u32[]{:S(2)}) copy-start(bf16[512,4096]{1,0:T(8,128)(2,1)} %copy-done.8) | copy-start | bytes 12582916
  62.7 24.4 %collective-permute-start.6 = (bf16[36,16,512]{2,1,0:T(8,128)(2,1)}, bf16[36,16,512]{2,1,0:T(8,128)(2,1)}, u32[]{:S(2)}, u32[]{:S(2)}) collective-permute-start(bf16[36,16,512]{2,1,0:T(8,128)(2,1)} %shard_map.217.refs_0_), channel_id=1, source_target_pairs={{0,1},{1,0},{2,3},{3,2},{4,5},{5,4},{6,7},{7,6},{8,9},{9,8},{10,11... | collective-permute-start | bytes 1769480 | tf_op jit(solution)/shard_map/ppermute | solution.py:127
  70.8 16.3 %collective-permute-start.10 = (bf16[28,16,512]{2,1,0:T(8,128)(2,1)}, bf16[28,16,512]{2,1,0:T(8,128)(2,1)}, u32[]{:S(2)}, u32[]{:S(2)}) collective-permute-start(bf16[28,16,512]{2,1,0:T(8,128)(2,1)} %shard_map.218), channel_id=1, source_target_pairs={{0,1},{1,0},{2,3},{3,2},{4,5},{5,4},{6,7},{7,6},{8,9},{9,8},{10,11... | collective-permute-start | bytes 1376264 | tf_op jit(solution)/shard_map/ppermute | solution.py:127
  70.8 17.8 %collective-permute-start.9 = (bf16[28,16,512]{2,1,0:T(8,128)(2,1)}, bf16[28,16,512]{2,1,0:T(8,128)(2,1)}, u32[]{:S(2)}, u32[]{:S(2)}) collective-permute-start(bf16[28,16,512]{2,1,0:T(8,128)(2,1)} %shard_map.218), channel_id=1, source_target_pairs={{0,15},{1,2},{2,1},{3,4},{4,3},{5,6},{6,5},{7,8},{8,7},{9,10},{10,... | collective-permute-start | bytes 1376264 | tf_op jit(solution)/shard_map/ppermute | solution.py:127
  76.3 2.9 %copy-start.18 = (s32[32,1]{1,0:T(8,128)S(1)}, s32[32,1]{1,0:T(8,128)}, u32[]{:S(2)}) copy-start(s32[32,1]{1,0:T(8,128)} %constant.186) | copy-start | bytes 388
  79.2 2.7 %copy-start.10 = (bf16[128,4096]{1,0:T(8,128)(2,1)S(1)}, bf16[128,4096]{1,0:T(8,128)(2,1)}, u32[]{:S(2)}) copy-start(bf16[128,4096]{1,0:T(8,128)(2,1)} %get-tuple-element.16) | copy-start | bytes 3145732
  79.4 3.7 %copy-start.17 = (s32[32,1]{1,0:T(8,128)S(1)}, s32[32,1]{1,0:T(8,128)}, u32[]{:S(2)}) copy-start(s32[32,1]{1,0:T(8,128)} %constant.176) | copy-start | bytes 388
  85.0 12.8 %collective-permute-start.7 = (bf16[36,16,512]{2,1,0:T(8,128)(2,1)}, bf16[36,16,512]{2,1,0:T(8,128)(2,1)S(1)}, u32[]{:S(2)}, u32[]{:S(2)}) collective-permute-start(bf16[36,16,512]{2,1,0:T(8,128)(2,1)} %shard_map.217.refs_0_), channel_id=1, source_target_pairs={{0,2},{1,15},{2,4},{3,1},{4,6},{5,3},{6,8},{7,5},{8,10},{9,7},{10,... | collective-permute-start | bytes 1769480 | tf_op jit(solution)/shard_map/ppermute | solution.py:127
  85.1 12.8 %collective-permute-start.8 = (bf16[36,16,512]{2,1,0:T(8,128)(2,1)}, bf16[36,16,512]{2,1,0:T(8,128)(2,1)S(1)}, u32[]{:S(2)}, u32[]{:S(2)}) collective-permute-start(bf16[36,16,512]{2,1,0:T(8,128)(2,1)} %collective-permute-done.5.refs_1_), channel_id=1, source_target_pairs={{0,1},{1,0},{2,3},{3,2},{4,5},{5,4},{6,7},{7,6},{8,9},{9,8},{10,11... | collective-permute-start | bytes 1769480 | tf_op jit(solution)/shard_map/ppermute | solution.py:127
  87.1 2.8 %copy-start.4 = (bf16[1024,512]{1,0:T(8,128)(2,1)S(1)}, bf16[1024,512]{1,0:T(8,128)(2,1)}, u32[]{:S(2)}) copy-start(bf16[1024,512]{1,0:T(8,128)(2,1)} %get-tuple-element.17.refs_9_.refs_7_) | copy-start | bytes 3145732
  87.1 2.8 %copy-start.5 = (bf16[512,1024]{1,0:T(8,128)(2,1)S(1)}, bf16[512,1024]{1,0:T(8,128)(2,1)}, u32[]{:S(2)}) copy-start(bf16[512,1024]{1,0:T(8,128)(2,1)} %get-tuple-element.19.refs_7_.refs_5_) | copy-start | bytes 3145732
  (7 other events, 8.6 us)

commit v2 on v1

v2 whole, which is shorter than its diff:
```python
import functools

import jax
import jax.numpy as jnp
import numpy as np
from jax import lax
from jax.experimental import pallas as pl
from jax.experimental.pallas import tpu as pltpu
from jax.sharding import PartitionSpec as P

TILE = 256


def block_kernel(layer, far, parts, aliased, idx_ref, band_ref, *refs):
    fields = []
    for count in parts:
        fields.append(refs[:count])
        refs = refs[count:]
    mix_ref, gain_ref, win_ref, bin_ref, wout_ref = refs[:5]
    refs = refs[5 + aliased:]
    out_ref, filtered, held = refs[:3]
    joined = list(refs[3:])

    whole = []
    for pieces in fields:
        if len(pieces) == 1:
            whole.append(pieces[0])
            continue
        target = joined.pop(0)

        @pl.when(pl.program_id(0) == 0)
        def _(pieces=pieces, target=target):
            at = 0
            for piece in pieces:
                target[at:at + piece.shape[0]] = piece[...]
                at += piece.shape[0]

        whole.append(target)
    self_ref, outer_ref, inner_ref = whole[:3]
    rows, cells, channels = out_ref.shape
    first = pl.program_id(0) * rows
    basis = mix_ref.shape[0]
    depth = (15 if far else 9) * cells
    order = [(outer_ref, 1), (self_ref, 0), (inner_ref, 2)]
    if far:
        order += [(whole[3], 3), (whole[4], 3)]

    def one_row(i, carry):
        at = (first + i) * 16
        pieces = [ref[idx_ref[at + 3 * kind + t]] for ref, kind in order for t in range(3)]
        picked = jnp.concatenate(pieces, axis=0)
        terms = jnp.dot(band_ref[i, :, :depth], picked, preferred_element_type=jnp.float32)
        total = terms[:cells] * mix_ref[0:1, :]
        for k in range(1, basis):
            total = total + terms[k * cells:(k + 1) * cells] * mix_ref[k:k + 1, :]
        place = pl.ds(pl.multiple_of(i * cells, cells), cells)
        filtered[place, :] = total
        held[place, :] = self_ref[idx_ref[at + 12]]
        return carry

    lax.fori_loop(0, rows, one_row, 0, unroll=2)
    value = filtered[...]
    centred = value - jnp.mean(value, axis=-1, keepdims=True)
    var = jnp.mean(centred * centred, axis=-1, keepdims=True)
    gain = gain_ref[layer:layer + 1, :]
    normed = (centred * lax.rsqrt(var + 1e-05) * gain).astype(jnp.bfloat16)
    pre = jnp.dot(normed, win_ref[...], preferred_element_type=jnp.float32)
    pre = pre + bin_ref[layer:layer + 1, :]
    hidden = jax.nn.gelu(pre, approximate=True).astype(jnp.bfloat16)
    update = jnp.dot(hidden, wout_ref[...], preferred_element_type=jnp.float32)
    out = (held[...].astype(jnp.float32) + update).astype(jnp.bfloat16)
    out_ref[...] = out.reshape(rows, cells, channels)


def run_block(layer, idx, band, starts, rows, fields, weights, into=None, out_rows=None):
    mix, gain, win, bias, wout = weights
    base, step = starts[0], starts[1] - starts[0]
    far = len(fields) == 5
    cells, channels = fields[0][0].shape[1:]
    whole = lambda a: pl.BlockSpec(a.shape, lambda g, s, n=a.ndim: (0,) * n)
    one = lambda a: pl.BlockSpec((None,) + a.shape[1:], lambda g, s: (layer, 0, 0))
    flat = [a for f in fields for a in f]
    tail = flat + [mix, gain, win, bias, wout]
    in_specs = [
        pl.BlockSpec(
            (pl.Element(rows), pl.Element(band.shape[1]), pl.Element(band.shape[2])),
            lambda g, s: (base + g * step, 0, 0),
        )
    ]
    in_specs += [whole(a) for a in flat]
    in_specs += [one(mix), whole(gain), one(win), whole(bias), one(wout)]
    if into is not None:
        tail.append(into)
        in_specs.append(pl.BlockSpec(memory_space=pl.ANY))
    if out_rows is None:
        out_rows, place = 2 * rows, lambda g, s: (g, 0, 0)
    else:
        place = lambda g, s: (base // rows + g * (step // rows), 0, 0)
    joined = [
        pltpu.VMEM((sum(a.shape[0] for a in f), cells, channels), jnp.bfloat16)
        for f in fields if len(f) > 1
    ]
    grid = pltpu.PrefetchScalarGridSpec(
        num_scalar_prefetch=1,
        grid=(2,),
        in_specs=in_specs,
        out_specs=pl.BlockSpec((rows, cells, channels), place),
        scratch_shapes=[
            pltpu.VMEM((rows * cells, channels), jnp.float32),
            pltpu.VMEM((rows * cells, channels), jnp.bfloat16),
        ] + joined,
    )
    flops = 2 * rows * cells * channels * (2 * 8 * 240 + 4 * win.shape[2])
    return pl.pallas_call(
        functools.partial(
            block_kernel, layer, far, tuple(len(f) for f in fields), 0 if into is None else 1
        ),
        out_shape=jax.ShapeDtypeStruct((out_rows, cells, channels), jnp.bfloat16),
        grid_spec=grid,
        input_output_aliases={} if into is None else {1 + len(tail): 0},
        cost_estimate=pl.CostEstimate(
            flops=flops, bytes_accessed=16 * 2**20, transcendentals=2 * rows * cells * 1024
        ),
        compiler_params=pltpu.CompilerParams(vmem_limit_bytes=44 * 2**20),
    )(idx, band, *tail)


def banded(filter_set, zonal_width, cells, sign):
    basis, lat, taps, offsets = filter_set.shape
    half = (offsets - 1) // 2
    d = jnp.arange(offsets, dtype=jnp.int32)
    support = jnp.abs(d - half)[None, :] <= zonal_width[:, None]
    masked = jnp.where(support[None, :, None, :], filter_set, jnp.zeros((), filter_set.dtype))
    masked = masked.transpose(1, 0, 2, 3).reshape(lat * basis, taps * offsets)
    col = jnp.arange(TILE, dtype=jnp.int32)
    piece, tap, m = col // (taps * cells), (col // cells) % taps, col % cells
    place = jnp.array([-1, 0, 1, -2, 2, 99], jnp.int32)[jnp.minimum(piece, 5)] * sign
    j = jnp.arange(cells, dtype=jnp.int32)
    want = place[None, :] * cells + m[None, :] - j[:, None] + half
    table = (
        (want[None, None] == d[None, :, None, None])
        & (tap[None, None, None, :] == jnp.arange(taps)[:, None, None, None])
    )
    table = table.astype(jnp.bfloat16).reshape(taps * offsets, cells * TILE)
    band = jnp.dot(masked, table, preferred_element_type=jnp.float32).astype(jnp.bfloat16)
    return band.reshape(lat, basis * cells, TILE)


def packed(rows, top, bottom, lat):
    return jnp.where(
        rows < top, rows, jnp.where(rows >= bottom, rows - bottom + top, rows + lat - bottom)
    )


def per_device(
    state, zonal_width, tap_rows, filters, basis_mix, norm_gain, weight_in, bias_in, weight_out
):
    lat, cells, channels = state.shape
    devices = lax.axis_size("lon")
    me = lax.axis_index("lon")
    sign = 1 - 2 * (me % 2)
    n = devices
    to_outer = [(i, (i - 1) % n if i % 2 == 0 else (i + 1) % n) for i in range(n)]
    to_inner = [(i, i ^ 1) for i in range(n)]
    to_far = [(i, (i + 2) % n if i % 2 == 0 else (i - 2) % n) for i in range(n)]
    send = lambda x, route: lax.ppermute(x, "lon", route)
    q = lat // 4
    ends = lambda x, a: jnp.concatenate([x[:a], x[lat - a:]], axis=0)

    def indices(rows, self_at, outer_at, inner_at, far_top):
        taps = jnp.concatenate([tap_rows[lo:hi] for lo, hi in rows], axis=0)
        own = jnp.asarray(np.concatenate([np.arange(lo, hi) for lo, hi in rows]), jnp.int32)
        far_at = packed(taps, far_top, lat - far_top, lat)
        far_at = jnp.clip(far_at, 0, 2 * far_top - 1)
        own = self_at(own)[:, None]
        pad = jnp.zeros((taps.shape[0], 3), jnp.int32)
        cols = [self_at(taps), outer_at(taps), inner_at(taps), far_at, own, pad]
        return jnp.concatenate(cols, axis=1).reshape(-1)

    weights = (basis_mix, norm_gain, weight_in, bias_in, weight_out)
    same = lambda r: r
    a, b = q + 4, q + 2
    at_a = lambda r: packed(r, a, lat - a, lat)
    at_b = lambda r: packed(r, b, lat - b, lat)
    mid_a, mid_q = (lat - 2 * b) // 2, (lat - 2 * q) // 2

    outer_p = send(ends(state, a), to_outer)
    far_out = send(ends(state, b), to_far)
    inner = send(state, to_inner)
    late, outer_p = lax.optimization_barrier((state[a:lat - a], outer_p))
    far_in = send(jnp.concatenate([outer_p[:b], outer_p[2 * a - b:]], axis=0), to_inner)
    outer_m = send(late, to_outer)
    band1, band2, idx1p, idx1m, idx2p, idx2m = lax.optimization_barrier((
        banded(filters[0], zonal_width, cells, sign),
        banded(filters[1], zonal_width, cells, sign),
        indices([(0, b), (lat - b, lat)], same, at_a, same, b),
        indices([(b, lat - b)], same, at_a, same, b),
        indices([(0, q), (lat - q, lat)], at_b, at_b, at_b, b),
        indices([(q, lat - q)], at_b, at_b, at_b, b),
    ))
    new_p = run_block(
        0, idx1p, band1, (0, lat - b), b,
        ((state,), (outer_p,), (inner,), (far_out,), (far_in,)), weights,
    )
    outer2_p = send(new_p, to_outer)
    far2_out = send(new_p, to_far)
    inner2_p = send(new_p, to_inner)
    new_m = run_block(
        0, idx1m, band1, (b, b + mid_a), mid_a,
        ((state,), (outer_p, outer_m), (inner,)), weights,
    )
    late2, outer2_p = lax.optimization_barrier((new_m, outer2_p))
    far2_in = send(outer2_p, to_inner)
    outer2_m = send(late2, to_outer)
    inner2_m = send(new_m, to_inner)
    out = run_block(
        1, idx2p, band2, (0, lat - q), q,
        ((new_p,), (outer2_p,), (inner2_p,), (far2_out,), (far2_in,)), weights, out_rows=lat,
    )
    return run_block(
        1, idx2m, band2, (q, q + mid_q), mid_q,
        ((new_p, new_m), (outer2_p, outer2_m), (inner2_p, inner2_m)), weights,
        into=out, out_rows=lat,
    )


def solution(mesh):
    placed = (P("parts", "lon", None), P(), P(), P(), P(), P(), P(), P(), P())
    return jax.shard_map(
        per_device, mesh=mesh, in_specs=placed, out_specs=P("parts", "lon", None), check_vma=False
    )
```

time: 108 us -> 136 us (1.26)
  waiting for transfers between devices: 1.72 us -> 30.6 us
  starting transfers between devices: 15.4 us -> 34.1 us
  local copies, waits for them, and re-layouts: 40.3 us -> 24.8 us
  other arithmetic: 14 us -> 4.82 us
  matrix products: 3.69 us -> 7.53 us
  Pallas kernels: 31.4 us -> 33.1 us
    ppermute x11, waiting for transfers between devices: 1.72 us -> 30.6 us  [per_device(): send = lambda x, route: lax.ppermute(x, 'lon', route)]
    slice x13 -> x2, local copies, waits for them, and re-layouts: 23.9 us -> 0.14 us  [indices(): taps = jnp.concatenate([tap_rows[lo:hi] for lo, hi in rows], axis=0)]
    ppermute x11, starting transfers between devices: 15.4 us -> 34.1 us  [per_device(): send = lambda x, route: lax.ppermute(x, 'lon', route)]
    reshape x4 -> x6, local copies, waits for them, and re-layouts: 0.44 us -> 15.3 us  [the longest x2 15 us: banded(): return band.reshape(lat, basis * cells, TILE)]
    concatenate x8 -> x0, other arithmetic: 10.6 us -> none  [the longest x1 2.08 us: per_device(): jnp.concatenate([state[:a], state[lat - a:], state[a:lat - a]], axis=0)]
    dot_general x2, matrix products: 3.69 us -> 7.53 us  [banded(): jnp.dot(masked, table, preferred_element_type=jnp.float32)]
    squeeze x3 -> x0, local copies, waits for them, and re-layouts: 2.3 us -> none  [the longest x1 1.18 us: weights(): weight_in[l]]
    gather x4 -> x0, local copies, waits for them, and re-layouts: 2.3 us -> none  [indices(): taps = tap_rows[rows]]
  transfers between devices with their start and end apart: 11 -> 11, of which waited for: 1 -> 2; matrix products, arithmetic and copies ran while one was open for 48% -> 25% of each run, Pallas kernels for 22% -> 12%
where the time goes in v2:
time: 136 us; the launch traced here: 135 us
  starting transfers between devices  34.1 us (25%)
  Pallas kernels  33.1 us (24%)
  waiting for transfers between devices  30.6 us (22%)
  local copies, waits for them, and re-layouts  24.8 us (18%)
  matrix products  7.53 us (6%)
  other arithmetic  4.82 us (4%)
    ppermute x11, starting transfers between devices, per_device(): send = lambda x, route: lax.ppermute(x, 'lon', route)  34.1 us
    pallas_call x4, Pallas kernels, run_block(): pl.pallas_call(functools.partial(block_kernel, layer, far, tuple((len(f)...  33.1 us
    ppermute x11, waiting for transfers between devices, per_device(): send = lambda x, route: lax.ppermute(x, 'lon', route)  30.6 us
    reshape x2, local copies, waits for them, and re-layouts, banded(): return band.reshape(lat, basis * cells, TILE)  15 us
    dot_general x2, matrix products, banded(): jnp.dot(masked, table, preferred_element_type=jnp.float32)  7.53 us
    unnamed x34, local copies, waits for them, and re-layouts  3.56 us
  transfers between devices with their start and end apart: 11, of which 2 were waited for; matrix products, arithmetic and copies ran while one was open for 25% of the time, Pallas kernels for 12%

profile of v2, /device:TPU:0, one launch (start us, length us, event | category | flops | bytes accessed | tf_op | source)
XLA Modules:
  0.0 135.2 jit_solution(299993467496114982)
XLA Ops:
  0.0 0.5 collective-permute-start.1
  0.5 1.1 fusion.10
  1.6 0.9 pad_maximum_fusion
  2.5 5.7 %collective-permute-start = (bf16[40,16,512]{2,1,0:T(8,128)(2,1)}, bf16[40,16,512]{2,1,0:T(8,128)(2,1)S(1)}, u32[]{:S(2)}, u32[]{:S(2)}) collective-permute-start(bf16[40,16,512]{2,1,0:T(8,128)(2,1)} %pad_maximum_fusion), channel_id=1, source_target_pairs={{0,15},{1,2},{2,1},{3,4},{4,3},{5,6},{6,5},{7,8},{8,7},{9,10},{10,... | collective-permute-start | bytes 1966088 | tf_op jit(solution)/shard_map/ppermute | solution.py:166
  8.1 1.1 fusion.9
  9.2 0.9 pad_maximum_fusion.1
  10.3 0.8 slice.53
  11.3 0.4 broadcast_and_fusion
  11.9 0.5 copy.23
  12.6 1.2 fusion
  13.7 0.3 copy.18
  14.1 1.0 reshape.251
  15.1 0.3 copy.17
  15.7 4.3 %convolution_convert_fusion = bf16[512,4096]{1,0:T(8,128)(2,1)} fusion(bf16[512,195]{1,0:T(8,128)(2,1)} %reshape.251, pred[195,4096]{1,0:T(8,128)(4,1)S(1)} %bitcast.23), kind=kOutput, calls=%fused_computation | convolution fusion | flops 819986432 | bytes 5192704 | tf_op jit(solution)/shard_map/dot_general | solution.py:145
  20.0 3.3 %convolution_convert_fusion.1 = bf16[512,4096]{1,0:T(8,128)(2,1)} fusion(bf16[512,195]{1,0:T(8,128)(2,1)S(1)} %reshape.249, pred[195,4096]{1,0:T(8,128)(4,1)S(1)} %bitcast.24), kind=kOutput, calls=%fused_computation.1 | convolution fusion | flops 819986432 | bytes 5192704 | tf_op jit(solution)/shard_map/dot_general | solution.py:145
  23.3 1.0 pad_maximum_fusion.2
  24.3 8.5 %collective-permute-start.3 = (bf16[36,16,512]{2,1,0:T(8,128)(2,1)}, bf16[36,16,512]{2,1,0:T(8,128)(2,1)}, u32[]{:S(2)}, u32[]{:S(2)}) collective-permute-start(bf16[36,16,512]{2,1,0:T(8,128)(2,1)} %pad_maximum_fusion.2), channel_id=1, source_target_pairs={{0,1},{1,0},{2,3},{3,2},{4,5},{5,4},{6,7},{7,6},{8,9},{9,8},{10,11... | collective-permute-start | bytes 1769480 | tf_op jit(solution)/shard_map/ppermute | solution.py:166
  32.8 7.4 %reshape.252.band_ref = bf16[64,128,256]{2,1,0:T(8,128)(2,1)} reshape(bf16[512,4096]{1,0:T(8,128)(2,1)} %convolution_convert_fusion) | data formatting | bytes 8388608 | tf_op jit(solution)/shard_map/reshape | solution.py:146
  40.2 7.6 %reshape.250.band_ref = bf16[64,128,256]{2,1,0:T(8,128)(2,1)} reshape(bf16[512,4096]{1,0:T(8,128)(2,1)} %convolution_convert_fusion.1) | data formatting | bytes 8388608 | tf_op jit(solution)/shard_map/reshape | solution.py:146
  49.3 1.6 %copy-done.1 = bf16[2,1024,512]{2,1,0:T(8,128)(2,1)S(1)} copy-done((bf16[2,1024,512]{2,1,0:T(8,128)(2,1)S(1)}, bf16[2,1024,512]{2,1,0:T(8,128)(2,1)}, u32[]{:S(2)}) %copy-start.1) | copy-done | bytes 2097176
  50.9 1.1 copy-done.5
  52.0 9.2 %shard_map.145.refs_0_ = bf16[36,16,512]{2,1,0:T(8,128)(2,1)S(1)} custom-call(s32[576]{0:T(1024)S(1)} %reshape.253.idx_ref, bf16[64,128,256]{2,1,0:T(8,128)(2,1)} %reshape.250.band_ref, bf16[64,16,512]{2,1,0:T(8,128)(2,1)S(1)} %copy-done.3, bf16[40,16,512]{2,1,0:T(8,128)(2,1)S(1)} %copy-done.5, bf16[64,16,512]{2,1,0:T(8,128)(2,1)} %collective-permute-done.1.refs_2_.refs_3_, ...), custom_call_target="tpu_custom_call" | custom-call | flops 2340421632 | bytes 16777216 | tf_op jit(solution)/shard_map/pallas_call | solution.py:114
  61.2 5.2 %collective-permute-start.5 = (bf16[36,16,512]{2,1,0:T(8,128)(2,1)S(1)}, bf16[36,16,512]{2,1,0:T(8,128)(2,1)S(1)}, u32[]{:S(2)}, u32[]{:S(2)}) collective-permute-start(bf16[36,16,512]{2,1,0:T(8,128)(2,1)S(1)} %shard_map.145.refs_0_), channel_id=1, source_target_pairs={{0,15},{1,2},{2,1},{3,4},{4,3},{5,6},{6,5},{7,8},{8,7},{9,10},{10,... | collective-permute-start | bytes 1769480 | tf_op jit(solution)/shard_map/ppermute | solution.py:166
  66.4 11.8 %collective-permute-done.4.refs_2_ = bf16[24,16,512]{2,1,0:T(8,128)(2,1)S(1)} collective-permute-done((bf16[24,16,512]{2,1,0:T(8,128)(2,1)S(1)}, bf16[24,16,512]{2,1,0:T(8,128)(2,1)S(1)}, u32[]{:S(2)}, u32[]{:S(2)}) %collective-permute-start.4) | collective-permute-done | bytes 393248 | tf_op jit(solution)/shard_map/ppermute | solution.py:166
  78.2 7.2 %shard_map.146.refs_1_ = bf16[28,16,512]{2,1,0:T(8,128)(2,1)S(1)} custom-call(s32[448]{0:T(512)S(1)} %reshape.254.idx_ref, bf16[64,128,256]{2,1,0:T(8,128)(2,1)} %reshape.250.band_ref, bf16[64,16,512]{2,1,0:T(8,128)(2,1)S(1)} %copy-done.3, bf16[40,16,512]{2,1,0:T(8,128)(2,1)S(1)} %copy-done.5, bf16[24,16,512]{2,1,0:T(8,128)(2,1)S(1)} %collective-permute-done.4.refs_2_, ...), custom_call_target="tpu_custom_call" | custom-call | flops 1820327936 | bytes 16777216 | tf_op jit(solution)/shard_map/pallas_call | solution.py:114
  85.4 7.8 %collective-permute-start.7 = (bf16[36,16,512]{2,1,0:T(8,128)(2,1)S(1)}, bf16[36,16,512]{2,1,0:T(8,128)(2,1)S(1)}, u32[]{:S(2)}, u32[]{:S(2)}) collective-permute-start(bf16[36,16,512]{2,1,0:T(8,128)(2,1)S(1)} %shard_map.145.refs_0_), channel_id=1, source_target_pairs={{0,1},{1,0},{2,3},{3,2},{4,5},{5,4},{6,7},{7,6},{8,9},{9,8},{10,11... | collective-permute-start | bytes 1769480 | tf_op jit(solution)/shard_map/ppermute | solution.py:166
  93.2 1.7 %collective-permute-start.9 = (bf16[36,16,512]{2,1,0:T(8,128)(2,1)S(1)}, bf16[36,16,512]{2,1,0:T(8,128)(2,1)S(1)}, u32[]{:S(2)}, u32[]{:S(2)}) collective-permute-start(bf16[36,16,512]{2,1,0:T(8,128)(2,1)S(1)} %shard_map.145.refs_0_), channel_id=1, source_target_pairs={{0,2},{1,15},{2,4},{3,1},{4,6},{5,3},{6,8},{7,5},{8,10},{9,7},{10,... | collective-permute-start | bytes 1769480 | tf_op jit(solution)/shard_map/ppermute | solution.py:166
  94.9 2.9 %collective-permute-start.10 = (bf16[36,16,512]{2,1,0:T(8,128)(2,1)S(1)}, bf16[36,16,512]{2,1,0:T(8,128)(2,1)S(1)}, u32[]{:S(2)}, u32[]{:S(2)}) collective-permute-start(bf16[36,16,512]{2,1,0:T(8,128)(2,1)S(1)} %collective-permute-done.5.refs_1_.refs_2_), channel_id=1, source_target_pairs={{0,1},{1,0},{2,3},{3,2},{4,5},{5,4},{6,7},{7,6},{8,9},{9,8},{10,11... | collective-permute-start | bytes 1769480 | tf_op jit(solution)/shard_map/ppermute | solution.py:166
  97.9 1.8 %collective-permute-start.6 = (bf16[28,16,512]{2,1,0:T(8,128)(2,1)S(1)}, bf16[28,16,512]{2,1,0:T(8,128)(2,1)S(1)}, u32[]{:S(2)}, u32[]{:S(2)}) collective-permute-start(bf16[28,16,512]{2,1,0:T(8,128)(2,1)S(1)} %shard_map.146.refs_1_), channel_id=1, source_target_pairs={{0,15},{1,2},{2,1},{3,4},{4,3},{5,6},{6,5},{7,8},{8,7},{9,10},{10,... | collective-permute-start | bytes 1376264 | tf_op jit(solution)/shard_map/ppermute | solution.py:166
  99.7 18.8 %collective-permute-done.9.refs_3_ = bf16[36,16,512]{2,1,0:T(8,128)(2,1)S(1)} collective-permute-done((bf16[36,16,512]{2,1,0:T(8,128)(2,1)S(1)}, bf16[36,16,512]{2,1,0:T(8,128)(2,1)S(1)}, u32[]{:S(2)}, u32[]{:S(2)}) %collective-permute-start.9) | collective-permute-done | bytes 589856 | tf_op jit(solution)/shard_map/ppermute | solution.py:166
  118.5 8.4 %shard_map.147.refs_11_ = bf16[64,16,512]{2,1,0:T(8,128)(2,1)} custom-call(s32[512]{0:T(512)S(1)} %reshape.255.idx_ref, bf16[64,128,256]{2,1,0:T(8,128)(2,1)} %reshape.252.band_ref, bf16[36,16,512]{2,1,0:T(8,128)(2,1)S(1)} %shard_map.145.refs_0_, bf16[36,16,512]{2,1,0:T(8,128)(2,1)S(1)} %collective-permute-done.5.refs_1_.refs_2_, ...), custom_call_target="tpu_custom_call" | custom-call | flops 2080374784 | bytes 16777216 | tf_op jit(solution)/shard_map/pallas_call | solution.py:114
  126.9 8.3 %shard_map.148 = bf16[64,16,512]{2,1,0:T(8,128)(2,1)} custom-call(s32[512]{0:T(512)S(1)} %reshape.256.idx_ref, bf16[64,128,256]{2,1,0:T(8,128)(2,1)} %reshape.252.band_ref, bf16[36,16,512]{2,1,0:T(8,128)(2,1)S(1)} %shard_map.145.refs_0_, bf16[28,16,512]{2,1,0:T(8,128)(2,1)S(1)} %shard_map.146.refs_1_, ...), custom_call_target="tpu_custom_call", output_to_operand_aliasing={{}: (13, {})} | custom-call | flops 2080374784 | bytes 16777216 | tf_op jit(solution)/shard_map/pallas_call | solution.py:114
  (75 shorter events, 2.6 us)
Async XLA Ops:
  0.0 10.3 %copy-start.3 = (bf16[64,16,512]{2,1,0:T(8,128)(2,1)S(1)}, bf16[64,16,512]{2,1,0:T(8,128)(2,1)}, u32[]{:S(2)}) copy-start(bf16[64,16,512]{2,1,0:T(8,128)(2,1)} %refs_0_.3) | copy-start | bytes 3145732
  0.0 10.1 %copy-start.10 = (s32[64,3]{0,1:T(4,128)S(1)}, s32[64,3]{0,1:T(4,128)}, u32[]{:S(2)}) copy-start(s32[64,3]{0,1:T(4,128)} %param.17) | copy-start | bytes 2308
  0.0 49.2 %collective-permute-start.1 = (bf16[64,16,512]{2,1,0:T(8,128)(2,1)}, bf16[64,16,512]{2,1,0:T(8,128)(2,1)}, u32[]{:S(2)}, u32[]{:S(2)}) collective-permute-start(bf16[64,16,512]{2,1,0:T(8,128)(2,1)} %refs_0_.3), channel_id=1, source_target_pairs={{0,1},{1,0},{2,3},{3,2},{4,5},{5,4},{6,7},{7,6},{8,9},{9,8},{10,11... | collective-permute-start | bytes 3145736 | tf_op jit(solution)/shard_map/ppermute | solution.py:166
  2.5 10.0 %copy-start.11 = (s32[64]{0:T(128)S(1)}, s32[64]{0:T(128)}, u32[]{:S(2)}) copy-start(s32[64]{0:T(128)} %param.16) | copy-start | bytes 772
  2.5 20.8 %collective-permute-start = (bf16[40,16,512]{2,1,0:T(8,128)(2,1)}, bf16[40,16,512]{2,1,0:T(8,128)(2,1)S(1)}, u32[]{:S(2)}, u32[]{:S(2)}) collective-permute-start(bf16[40,16,512]{2,1,0:T(8,128)(2,1)} %pad_maximum_fusion), channel_id=1, source_target_pairs={{0,15},{1,2},{2,1},{3,4},{4,3},{5,6},{6,5},{7,8},{8,7},{9,10},{10,... | collective-permute-start | bytes 1966088 | tf_op jit(solution)/shard_map/ppermute | solution.py:166
  10.1 39.1 %collective-permute-start.2 = (bf16[36,16,512]{2,1,0:T(8,128)(2,1)}, bf16[36,16,512]{2,1,0:T(8,128)(2,1)}, u32[]{:S(2)}, u32[]{:S(2)}) collective-permute-start(bf16[36,16,512]{2,1,0:T(8,128)(2,1)} %pad_maximum_fusion.1), channel_id=1, source_target_pairs={{0,2},{1,15},{2,4},{3,1},{4,6},{5,3},{6,8},{7,5},{8,10},{9,7},{10,... | collective-permute-start | bytes 1769480 | tf_op jit(solution)/shard_map/ppermute | solution.py:166
  23.3 9.5 %copy-start.4 = (bf16[40,16,512]{2,1,0:T(8,128)(2,1)}, bf16[40,16,512]{2,1,0:T(8,128)(2,1)S(1)}, u32[]{:S(2)}) copy-start(bf16[40,16,512]{2,1,0:T(8,128)(2,1)S(1)} %collective-permute-done.refs_1_) | copy-start | bytes 1966084
  24.3 25.0 %collective-permute-start.3 = (bf16[36,16,512]{2,1,0:T(8,128)(2,1)}, bf16[36,16,512]{2,1,0:T(8,128)(2,1)}, u32[]{:S(2)}, u32[]{:S(2)}) collective-permute-start(bf16[36,16,512]{2,1,0:T(8,128)(2,1)} %pad_maximum_fusion.2), channel_id=1, source_target_pairs={{0,1},{1,0},{2,3},{3,2},{4,5},{5,4},{6,7},{7,6},{8,9},{9,8},{10,11... | collective-permute-start | bytes 1769480 | tf_op jit(solution)/shard_map/ppermute | solution.py:166
  40.2 7.7 %copy-start.15 = (s32[36,1]{0,1:T(1,128)S(1)}, s32[36,1]{0,1:T(1,128)}, u32[]{:S(2)}) copy-start(s32[36,1]{0,1:T(1,128)} %constant.159) | copy-start | bytes 436
  40.2 8.0 %copy-start.14 = (s32[32,1]{0,1:T(1,128)S(1)}, s32[32,1]{0,1:T(1,128)}, u32[]{:S(2)}) copy-start(s32[32,1]{0,1:T(1,128)} %constant.167) | copy-start | bytes 388
  40.2 8.4 %copy-start.13 = (s32[28,1]{0,1:T(1,128)S(1)}, s32[28,1]{0,1:T(1,128)}, u32[]{:S(2)}) copy-start(s32[28,1]{0,1:T(1,128)} %constant.160) | copy-start | bytes 340
  40.2 8.8 %copy-start.12 = (s32[32,1]{0,1:T(1,128)S(1)}, s32[32,1]{0,1:T(1,128)}, u32[]{:S(2)}) copy-start(s32[32,1]{0,1:T(1,128)} %constant.174) | copy-start | bytes 388
  40.2 9.1 %copy-start = (bf16[2,512,1024]{2,1,0:T(8,128)(2,1)S(1)}, bf16[2,512,1024]{2,1,0:T(8,128)(2,1)}, u32[]{:S(2)}) copy-start(bf16[2,512,1024]{2,1,0:T(8,128)(2,1)} %refs_8_.7) | copy-start | bytes 6291460
  40.2 9.1 %copy-start.6 = (f32[2,8,512]{2,1,0:T(8,128)S(1)}, f32[2,8,512]{2,1,0:T(8,128)}, u32[]{:S(2)}) copy-start(f32[2,8,512]{2,1,0:T(8,128)} %refs_6_.7) | copy-start | bytes 98308
  40.2 9.1 %copy-start.7 = (f32[2,1024]{1,0:T(2,128)S(1)}, f32[2,1024]{1,0:T(2,128)}, u32[]{:S(2)}) copy-start(f32[2,1024]{1,0:T(2,128)} %refs_9_.5) | copy-start | bytes 24580
  40.2 9.1 %copy-start.8 = (f32[2,512]{1,0:T(2,128)S(1)}, f32[2,512]{1,0:T(2,128)}, u32[]{:S(2)}) copy-start(f32[2,512]{1,0:T(2,128)} %refs_7_.7) | copy-start | bytes 12292
  49.3 1.6 %copy-start.1 = (bf16[2,1024,512]{2,1,0:T(8,128)(2,1)S(1)}, bf16[2,1024,512]{2,1,0:T(8,128)(2,1)}, u32[]{:S(2)}) copy-start(bf16[2,1024,512]{2,1,0:T(8,128)(2,1)} %refs_10_.1) | copy-start | bytes 6291460
  50.9 1.1 copy-start.5
  52.0 14.4 %copy-start.9 = (bf16[24,16,512]{2,1,0:T(8,128)(2,1)S(1)}, bf16[24,16,512]{2,1,0:T(8,128)(2,1)}, u32[]{:S(2)}) copy-start(bf16[24,16,512]{2,1,0:T(8,128)(2,1)} %slice.53) | copy-start | bytes 1179652
  52.0 26.3 %copy-start.2 = (bf16[2,1024,512]{2,1,0:T(8,128)(2,1)S(1)}, bf16[2,1024,512]{2,1,0:T(8,128)(2,1)}, u32[]{:S(2)}) copy-start(bf16[2,1024,512]{2,1,0:T(8,128)(2,1)} %refs_10_.1) | copy-start | bytes 6291460
  61.2 33.7 %collective-permute-start.5 = (bf16[36,16,512]{2,1,0:T(8,128)(2,1)S(1)}, bf16[36,16,512]{2,1,0:T(8,128)(2,1)S(1)}, u32[]{:S(2)}, u32[]{:S(2)}) collective-permute-start(bf16[36,16,512]{2,1,0:T(8,128)(2,1)S(1)} %shard_map.145.refs_0_), channel_id=1, source_target_pairs={{0,15},{1,2},{2,1},{3,4},{4,3},{5,6},{6,5},{7,8},{8,7},{9,10},{10,... | collective-permute-start | bytes 1769480 | tf_op jit(solution)/shard_map/ppermute | solution.py:166
  66.4 11.9 %collective-permute-start.4 = (bf16[24,16,512]{2,1,0:T(8,128)(2,1)S(1)}, bf16[24,16,512]{2,1,0:T(8,128)(2,1)S(1)}, u32[]{:S(2)}, u32[]{:S(2)}) collective-permute-start(bf16[24,16,512]{2,1,0:T(8,128)(2,1)S(1)} %copy-done.9), channel_id=1, source_target_pairs={{0,15},{1,2},{2,1},{3,4},{4,3},{5,6},{6,5},{7,8},{8,7},{9,10},{10,... | collective-permute-start | bytes 1179656 | tf_op jit(solution)/shard_map/ppermute | solution.py:166
  85.4 14.2 %collective-permute-start.7 = (bf16[36,16,512]{2,1,0:T(8,128)(2,1)S(1)}, bf16[36,16,512]{2,1,0:T(8,128)(2,1)S(1)}, u32[]{:S(2)}, u32[]{:S(2)}) collective-permute-start(bf16[36,16,512]{2,1,0:T(8,128)(2,1)S(1)} %shard_map.145.refs_0_), channel_id=1, source_target_pairs={{0,1},{1,0},{2,3},{3,2},{4,5},{5,4},{6,7},{7,6},{8,9},{9,8},{10,11... | collective-permute-start | bytes 1769480 | tf_op jit(solution)/shard_map/ppermute | solution.py:166
  93.2 25.3 %collective-permute-start.9 = (bf16[36,16,512]{2,1,0:T(8,128)(2,1)S(1)}, bf16[36,16,512]{2,1,0:T(8,128)(2,1)S(1)}, u32[]{:S(2)}, u32[]{:S(2)}) collective-permute-start(bf16[36,16,512]{2,1,0:T(8,128)(2,1)S(1)} %shard_map.145.refs_0_), channel_id=1, source_target_pairs={{0,2},{1,15},{2,4},{3,1},{4,6},{5,3},{6,8},{7,5},{8,10},{9,7},{10,... | collective-permute-start | bytes 1769480 | tf_op jit(solution)/shard_map/ppermute | solution.py:166
  94.9 23.6 %collective-permute-start.10 = (bf16[36,16,512]{2,1,0:T(8,128)(2,1)S(1)}, bf16[36,16,512]{2,1,0:T(8,128)(2,1)S(1)}, u32[]{:S(2)}, u32[]{:S(2)}) collective-permute-start(bf16[36,16,512]{2,1,0:T(8,128)(2,1)S(1)} %collective-permute-done.5.refs_1_.refs_2_), channel_id=1, source_target_pairs={{0,1},{1,0},{2,3},{3,2},{4,5},{5,4},{6,7},{7,6},{8,9},{9,8},{10,11... | collective-permute-start | bytes 1769480 | tf_op jit(solution)/shard_map/ppermute | solution.py:166
  97.9 29.0 %collective-permute-start.8 = (bf16[28,16,512]{2,1,0:T(8,128)(2,1)S(1)}, bf16[28,16,512]{2,1,0:T(8,128)(2,1)S(1)}, u32[]{:S(2)}, u32[]{:S(2)}) collective-permute-start(bf16[28,16,512]{2,1,0:T(8,128)(2,1)S(1)} %shard_map.146.refs_1_), channel_id=1, source_target_pairs={{0,1},{1,0},{2,3},{3,2},{4,5},{5,4},{6,7},{7,6},{8,9},{9,8},{10,11... | collective-permute-start | bytes 1376264 | tf_op jit(solution)/shard_map/ppermute | solution.py:166
  97.9 29.0 %collective-permute-start.6 = (bf16[28,16,512]{2,1,0:T(8,128)(2,1)S(1)}, bf16[28,16,512]{2,1,0:T(8,128)(2,1)S(1)}, u32[]{:S(2)}, u32[]{:S(2)}) collective-permute-start(bf16[28,16,512]{2,1,0:T(8,128)(2,1)S(1)} %shard_map.146.refs_1_), channel_id=1, source_target_pairs={{0,15},{1,2},{2,1},{3,4},{4,3},{5,6},{6,5},{7,8},{8,7},{9,10},{10,... | collective-permute-start | bytes 1376264 | tf_op jit(solution)/shard_map/ppermute | solution.py:166
